TPU v7x, 512 devices: a whole 4x8x8 slice. The times are simulated.
512 devices in a mesh: dp: 32 (over x, y_lo, core), mp: 16 (over y_hi, z).
Axes of the slice: x: 4, y: 8 (y_hi: 2, y_lo: 4; y = y_hi * 4 + y_lo), z: 8, core: 2. Of those that a mesh axis runs over, the one named last changes fastest.
Arguments:
- inputs: bfloat16 [2048, 8192], P('dp', 'mp'), may hold values from -6 to 6
- block_weights: bfloat16 [16, 5, 2048, 512], P('mp', None, 'dp'), may hold values from -0.125 to 0.125
- partners: int32 [16, 5], P('mp'), may hold values from 0 to 15, as said below
- code_in: bfloat16 [8192, 256], P('mp'), may hold values from -0.0625 to 0.0625
- code_out: bfloat16 [256, 16, 2048], P(None, 'mp', 'dp'), may hold values from -0.375 to 0.375
- upstream: bfloat16 [16, 2048, 2048], P('mp', None, 'dp'), may hold values from -1.5 to 1.5
Outputs:
- input_grad: bfloat16 [2048, 8192], P('dp', 'mp')
- block_grad: float32 [16, 5, 2048, 512], P('mp', None, 'dp')
- code_in_grad: float32 [8192, 256], P('mp')
- code_out_grad: float32 [256, 16, 2048], P(None, 'mp', 'dp')
Inputs may be any that keep to these rules, and one draw needn't show every extreme that they name: Row i of partners lists the 5 hidden blocks i and i xor 2^k for k = 0 to 3, each once, in some order.
All inputs are finite; a program needn't handle non-finite values.
Results may differ from a plain program's by a relative error of at most 0.0059.
Values may be sent and summed in bfloat16 or wider, within the bound.
No kernel may reach another device: no remote copies, remote signals or barrier semaphores. Data moves between devices by JAX's collectives and lax.ppermute only.
A program may use at most 64 MiB of HBM per device.

v0:
```python
import jax
import jax.numpy as jnp
from jax import lax
from jax.sharding import PartitionSpec as P


def from_partner(block, axis, stride):
    count = lax.axis_size(axis)
    route = []
    for low in range(count):
        high = low | 1 << stride
        if high != low and high < count:
            route += [(low, high), (high, low)]
    return lax.ppermute(block, axis, route)


def gelu_slope(pre):
    return (
        0.5 * (1.0 + lax.erf(pre * 0.7071067811865476))
        + pre * jnp.exp(-0.5 * pre * pre) * 0.3989422804014327
    )


def body(inputs, block_weights, partners, code_in, code_out, upstream):
    local = block_weights.shape[0]
    slots = block_weights.shape[1]
    block_rows = block_weights.shape[3]
    first = lax.axis_index("mp") * local
    row_ids = first + jnp.arange(local, dtype=jnp.int32)
    masks = [0] + [1 << k for k in range(slots - 1)]
    targets = jnp.bitwise_xor(row_ids[:, None], jnp.array(masks, jnp.int32)[None, :])
    select = (partners[:, None, :] == targets[:, :, None]).astype(jnp.bfloat16)
    by_kind = jnp.einsum(
        "aqs,asck->aqck", select, block_weights, preferred_element_type=jnp.float32
    ).astype(jnp.bfloat16)
    own_codes = jnp.dot(inputs, code_in, preferred_element_type=jnp.float32)
    own_codes = lax.psum(own_codes, "mp").astype(jnp.bfloat16)
    gathered, codes = (
        lax.all_gather(inputs, "dp", axis=0, tiled=True),
        lax.all_gather(own_codes, "dp", axis=0, tiled=True),
    )
    tokens = gathered.shape[0]
    gathered_blocks = gathered.reshape(tokens, local, block_rows)
    products = jnp.einsum(
        "tak,aqck->qact", gathered_blocks, by_kind, preferred_element_type=jnp.float32
    )
    hidden = products[0]
    for kind in range(1, slots):
        mask = masks[kind]
        term = products[kind].astype(jnp.bfloat16)
        arrived = from_partner(term, "mp", (mask // local).bit_length() - 1)
        hidden = hidden + arrived.astype(jnp.float32)
    hidden = hidden + jnp.einsum("tr,rac->act", codes, code_out, preferred_element_type=jnp.float32)
    slopes_in = lax.all_to_all(upstream, "dp", split_axis=1, concat_axis=2, tiled=True)
    dpre = (slopes_in.astype(jnp.float32) * gelu_slope(hidden)).astype(jnp.bfloat16)
    kinds = [dpre]
    for kind in range(1, slots):
        mask = masks[kind]
        kinds.append(from_partner(dpre, "mp", (mask // local).bit_length() - 1))
    stacked = jnp.stack(kinds, axis=0)
    back = jnp.einsum("act,rac->tr", dpre, code_out, preferred_element_type=jnp.float32)
    back = lax.psum(back, "mp").astype(jnp.bfloat16)
    partial_grad = jnp.einsum(
        "qact,aqck->tak", stacked, by_kind, preferred_element_type=jnp.float32
    )
    partial_grad = partial_grad.reshape(tokens, local * block_rows)
    partial_grad = partial_grad + jnp.einsum(
        "tr,kr->tk", back, code_in, preferred_element_type=jnp.float32
    )
    input_grad = lax.psum_scatter(partial_grad, "dp", scatter_dimension=0, tiled=True).astype(
        jnp.bfloat16
    )
    by_slot = jnp.einsum(
        "aqs,qact->asct", select, stacked, preferred_element_type=jnp.float32
    ).astype(jnp.bfloat16)
    block_grad = jnp.einsum(
        "asct,tak->asck", by_slot, gathered_blocks, preferred_element_type=jnp.float32
    )
    code_in_grad = jnp.einsum("tk,tr->kr", gathered, back, preferred_element_type=jnp.float32)
    code_in_grad = lax.psum(code_in_grad, "dp")
    code_out_grad = jnp.einsum("tr,act->rac", codes, dpre, preferred_element_type=jnp.float32)
    return (input_grad, block_grad, code_in_grad, code_out_grad)


def solution(mesh):
    in_specs = (
        P("dp", "mp"),
        P("mp", None, "dp", None),
        P("mp", None),
        P("mp", None),
        P(None, "mp", "dp"),
        P("mp", None, "dp"),
    )
    out_specs = (P("dp", "mp"), P("mp", None, "dp", None), P("mp", None), P(None, "mp", "dp"))
    return jax.shard_map(body, mesh=mesh, in_specs=in_specs, out_specs=out_specs, check_vma=False)
```

profile of v0, /device:TPU:64, one launch (start us, length us, event | category | flops | bytes accessed | tf_op | source)
XLA Modules:
  0.0 779.8 jit_solution(17467582253655647755)
XLA Ops:
  8.0 1.2 fusion.46
  9.1 97.5 %psum.21 = bf16[64,256]{1,0:T(8,128)(2,1)} all-reduce(f32[64,256]{1,0:T(8,128)S(1)} %fusion.46), channel_id=1, replica_groups=mesh['dp'=32,'mp'=16] {'mp'}, use_global_device_ids=true, to_apply=%region_0.0 | all-reduce | flops 16384 | bytes 98304 | tf_op jit(solution)/shard_map/psum | solution.py:37
  106.6 2.2 copy.29
  109.4 11.5 %reduce = bf16[2048,64]{1,0:T(8,128)(2,1)S(1)} reduce(bf16[2048,1,64]{2,1,0:T(2,128)(2,1)S(1)} %bitcast.83, bf16[]{:T(256)} %broadcast.19), dimensions={1}, to_apply=%bitcast.65.reduce_sub_computation | reduce | bytes 524290
  120.9 1.1 reshape.134
  122.0 4.8 all-to-all-start
  127.4 9.9 %all-to-all-done = bf16[32,2,2048]{2,1,0:T(2,128)(2,1)S(1)} async-done(((bf16[32,2,2048]{2,1,0:T(2,128)(2,1)}), bf16[32,2,2048]{2,1,0:T(2,128)(2,1)S(1)}, u32[]{:S(2)}, u32[]{:S(2)}) %all-to-all-start) | async-done | bytes 262176 | tf_op jit(solution)/shard_map/all_to_all | solution.py:54
  137.9 4.0 fusion.43
  142.0 10.2 %collective-permute-start = (bf16[1,64,2048]{2,1,0:T(8,128)(2,1)S(1)}, bf16[1,64,2048]{2,1,0:T(8,128)(2,1)}, u32[]{:S(2)}, u32[]{:S(2)}) collective-permute-start(bf16[1,64,2048]{2,1,0:T(8,128)(2,1)S(1)} %get-tuple-element.16), channel_id=1, source_target_pairs={{0,1},{1,0},{2,3},{3,2},{4,5},{5,4},{6,7},{7,6},{8,9},{9,8},{10,11... | collective-permute-start | bytes 786440 | tf_op jit(solution)/shard_map/ppermute | solution.py:14
  152.2 4.7 collective-permute-start.3
  156.9 1.9 collective-permute-start.2
  158.9 1.9 collective-permute-start.1
  160.8 1.1 bitcast_convert_fusion
  162.9 6.8 all-gather.5.cloned.1.call-done
  169.7 3.7 collective-permute-done.3
  173.6 6.8 collective-permute-done.1
  180.4 2.9 bitcast_dynamic-update-slice_fusion.4
  183.3 5.0 collective-permute-start.7
  188.3 7.1 collective-permute-start.6
  195.5 5.4 collective-permute-start.5
  200.9 1.9 collective-permute-start.4
  202.8 2.8 fusion.27
  205.6 123.1 %all-reduce.4 = bf16[2048,256]{1,0:T(8,128)(2,1)S(1)} all-reduce(f32[2048,256]{1,0:T(8,128)} %fusion.27), channel_id=1, replica_groups=mesh['dp'=32,'mp'=16] {'mp'}, use_global_device_ids=true, to_apply=%region_1.0 | all-reduce | flops 524288 | bytes 3145728 | tf_op jit(solution)/shard_map/psum | solution.py:62
  328.7 3.2 convolution_bitcast_fusion.1
  336.6 3.3 bitcast_add_fusion
  339.9 5.4 copy.39
  345.3 1.2 copy-done.3
  346.5 1.9 convolution_bitcast_fusion.2
  350.0 2.0 fusion.6
  352.0 261.3 %all-reduce.3.cloned.1.call-done = f32[512,256]{0,1:T(8,128)} async-done(((f32[512,256]{0,1:T(8,128)}), f32[512,256]{0,1:T(8,128)}) %all-reduce.3.cloned.1.call-update) | async-done | bytes 524304 | tf_op jit(solution)/shard_map/psum | solution.py:80
  613.3 2.0 copy.35
  615.3 156.2 %reduce-scatter.4.cloned.1.call-done = f32[64,512]{1,0:T(8,128)} async-done(((f32[2048,512]{1,0:T(8,128)}), f32[64,512]{1,0:T(8,128)}) %reduce-scatter.4.cloned.1.call-update) | async-done | bytes 131088
  (43 shorter events, 11.8 us)
Async XLA Ops:
  7.2 119.8 %copy-start = (bf16[1,5,64,512]{3,2,1,0:T(8,128)(2,1)S(1)}, bf16[1,5,64,512]{3,2,1,0:T(8,128)(2,1)}, u32[]{:S(2)}) copy-start(bf16[1,5,64,512]{3,2,1,0:T(8,128)(2,1)} %param.8) | copy-start | bytes 983044
  7.2 130.7 %all-gather.3.cloned.1.call-start = ((), (), s32[]{:S(2)}) async-start(), calls=%async_computation.2 | async-start | bytes 2162688 | tf_op jit(solution)/shard_map/all_gather | solution.py:39
  7.9 161.8 %all-gather.5.cloned.1.call-start = ((), (), s32[]{:S(2)}) async-start(), calls=%async_computation.3 | async-start | bytes 1081344 | tf_op jit(solution)/shard_map/all_gather | solution.py:40
  106.6 20.3 %copy-start.6 = (s32[5]{0:T(128)S(1)}, s32[5]{0:T(128)}, u32[]{:S(2)}) copy-start(s32[5]{0:T(128)} %constant.16.clone) | copy-start | bytes 64
  106.6 20.3 %copy-start.5 = (s32[1,5]{1,0:T(1,128)S(1)}, s32[1,5]{1,0:T(1,128)}, u32[]{:S(2)}) copy-start(s32[1,5]{1,0:T(1,128)} %param.9) | copy-start | bytes 64
  122.0 15.2 %all-to-all-start = ((bf16[32,2,2048]{2,1,0:T(2,128)(2,1)}), bf16[32,2,2048]{2,1,0:T(2,128)(2,1)S(1)}, u32[]{:S(2)}, u32[]{:S(2)}) async-start(bf16[32,2,2048]{2,1,0:T(2,128)(2,1)} %reshape.134), calls=%async_computation | async-start | bytes 524288 | tf_op jit(solution)/shard_map/all_to_all | solution.py:54
  126.9 486.4 %all-reduce.3.cloned.1.call-start = ((), (), s32[]{:S(2)}) async-start(), calls=%async_computation.4 | async-start | bytes 1048576 | tf_op jit(solution)/shard_map/psum | solution.py:80
  142.0 27.7 %collective-permute-start = (bf16[1,64,2048]{2,1,0:T(8,128)(2,1)S(1)}, bf16[1,64,2048]{2,1,0:T(8,128)(2,1)}, u32[]{:S(2)}, u32[]{:S(2)}) collective-permute-start(bf16[1,64,2048]{2,1,0:T(8,128)(2,1)S(1)} %get-tuple-element.16), channel_id=1, source_target_pairs={{0,1},{1,0},{2,3},{3,2},{4,5},{5,4},{6,7},{7,6},{8,9},{9,8},{10,11... | collective-permute-start | bytes 786440 | tf_op jit(solution)/shard_map/ppermute | solution.py:14
  152.2 21.2 %collective-permute-start.3 = (bf16[1,64,2048]{2,1,0:T(8,128)(2,1)S(1)}, bf16[1,64,2048]{2,1,0:T(8,128)(2,1)}, u32[]{:S(2)}, u32[]{:S(2)}) collective-permute-start(bf16[1,64,2048]{2,1,0:T(8,128)(2,1)S(1)} %get-tuple-element.17), channel_id=1, source_target_pairs={{0,8},{8,0},{1,9},{9,1},{2,10},{10,2},{3,11},{11,3},{4,12},{12,4},... | collective-permute-start | bytes 786440 | tf_op jit(solution)/shard_map/ppermute | solution.py:14
  156.9 16.7 %collective-permute-start.2 = (bf16[1,64,2048]{2,1,0:T(8,128)(2,1)S(1)}, bf16[1,64,2048]{2,1,0:T(8,128)(2,1)}, u32[]{:S(2)}, u32[]{:S(2)}) collective-permute-start(bf16[1,64,2048]{2,1,0:T(8,128)(2,1)S(1)} %get-tuple-element.18), channel_id=1, source_target_pairs={{0,4},{4,0},{1,5},{5,1},{2,6},{6,2},{3,7},{7,3},{8,12},{12,8},{9,1... | collective-permute-start | bytes 786440 | tf_op jit(solution)/shard_map/ppermute | solution.py:14
  158.9 21.5 %collective-permute-start.1 = (bf16[1,64,2048]{2,1,0:T(8,128)(2,1)S(1)}, bf16[1,64,2048]{2,1,0:T(8,128)(2,1)}, u32[]{:S(2)}, u32[]{:S(2)}) collective-permute-start(bf16[1,64,2048]{2,1,0:T(8,128)(2,1)S(1)} %get-tuple-element.19), channel_id=1, source_target_pairs={{0,2},{2,0},{1,3},{3,1},{4,6},{6,4},{5,7},{7,5},{8,10},{10,8},{9,1... | collective-permute-start | bytes 786440 | tf_op jit(solution)/shard_map/ppermute | solution.py:14
  161.9 18.5 %copy-start.4 = (bf16[256,1,64]{0,2,1:T(8,128)(2,1)S(1)}, bf16[256,1,64]{0,2,1:T(8,128)(2,1)}, u32[]{:S(2)}) copy-start(bf16[256,1,64]{0,2,1:T(8,128)(2,1)} %param.11) | copy-start | bytes 98308
  183.3 152.3 %collective-permute-start.7 = (bf16[1,64,2048]{2,1,0:T(8,128)(2,1)}, bf16[1,64,2048]{2,1,0:T(8,128)(2,1)}, u32[]{:S(2)}, u32[]{:S(2)}) collective-permute-start(bf16[1,64,2048]{2,1,0:T(8,128)(2,1)} %get-tuple-element.23), channel_id=1, source_target_pairs={{0,8},{8,0},{1,9},{9,1},{2,10},{10,2},{3,11},{11,3},{4,12},{12,4},... | collective-permute-start | bytes 786440 | tf_op jit(solution)/shard_map/ppermute | solution.py:14
  188.3 146.3 %collective-permute-start.6 = (bf16[1,64,2048]{2,1,0:T(8,128)(2,1)}, bf16[1,64,2048]{2,1,0:T(8,128)(2,1)}, u32[]{:S(2)}, u32[]{:S(2)}) collective-permute-start(bf16[1,64,2048]{2,1,0:T(8,128)(2,1)} %get-tuple-element.23), channel_id=1, source_target_pairs={{0,4},{4,0},{1,5},{5,1},{2,6},{6,2},{3,7},{7,3},{8,12},{12,8},{9,1... | collective-permute-start | bytes 786440 | tf_op jit(solution)/shard_map/ppermute | solution.py:14
  195.5 138.2 %collective-permute-start.5 = (bf16[1,64,2048]{2,1,0:T(8,128)(2,1)}, bf16[1,64,2048]{2,1,0:T(8,128)(2,1)}, u32[]{:S(2)}, u32[]{:S(2)}) collective-permute-start(bf16[1,64,2048]{2,1,0:T(8,128)(2,1)} %get-tuple-element.23), channel_id=1, source_target_pairs={{0,2},{2,0},{1,3},{3,1},{4,6},{6,4},{5,7},{7,5},{8,10},{10,8},{9,1... | collective-permute-start | bytes 786440 | tf_op jit(solution)/shard_map/ppermute | solution.py:14
  200.9 131.8 %collective-permute-start.4 = (bf16[1,64,2048]{2,1,0:T(8,128)(2,1)}, bf16[1,64,2048]{2,1,0:T(8,128)(2,1)}, u32[]{:S(2)}, u32[]{:S(2)}) collective-permute-start(bf16[1,64,2048]{2,1,0:T(8,128)(2,1)} %get-tuple-element.23), channel_id=1, source_target_pairs={{0,1},{1,0},{2,3},{3,2},{4,5},{5,4},{6,7},{7,6},{8,9},{9,8},{10,11... | collective-permute-start | bytes 786440 | tf_op jit(solution)/shard_map/ppermute | solution.py:14
  328.7 3.2 copy-start.2
  331.9 439.6 %reduce-scatter.4.cloned.1.call-start = ((), (), s32[]{:S(2)}) async-start(), calls=%async_computation.5 | async-start | bytes 4325376
  345.3 1.2 copy-start.3
  348.4 1.6 copy-start.1
Sparse Core Ops, SparseCore 0:
  10.2 66.6 all-gather.2
  106.7 62.9 all-gather.4
  332.0 281.2 all-reduce.2
  616.2 155.2 reduce-scatter.3
where the time goes:
time: 781 us; the launch traced here: 780 us
  waiting for transfers between devices  446 us (57%)
  blocking collectives  221 us (28%)
  starting transfers between devices  43.2 us (6%)
  matrix products  23.3 us (3%)
  local copies, waits for them, and re-layouts  20.4 us (3%)
  between operations  14 us (2%)
  other arithmetic  12.7 us (2%)
    psum x1, waiting for transfers between devices, body(): code_in_grad = lax.psum(code_in_grad, 'dp')  261 us
    unnamed x5, waiting for transfers between devices  157 us
    psum x1, blocking collectives, body(): back = lax.psum(back, 'mp').astype(jnp.bfloat16)  123 us
    psum x1, blocking collectives, body(): own_codes = lax.psum(own_codes, 'mp').astype(jnp.bfloat16)  97.5 us
    ppermute x8, starting transfers between devices, from_partner(): return lax.ppermute(block, axis, route)  38.2 us
    unnamed x25, local copies, waits for them, and re-layouts  18.4 us
  transfers between devices with their start and end apart: 13, of which 7 were waited for; matrix products, arithmetic and copies ran while one was open for 6% of the time, Pallas kernels for 0%

commit v1 on v0

v1 whole, which is shorter than its diff:
```python
import jax
import jax.numpy as jnp
from jax import lax
from jax.sharding import Mesh, PartitionSpec as P

F32 = jnp.float32
BF16 = jnp.bfloat16
X, Y, C, H, Z = 4, 4, 2, 2, 8
MASKS = (0, 1, 2, 4, 8)


def gelu_slope(pre):
    return (
        0.5 * (1.0 + lax.erf(pre * 0.7071067811865476))
        + pre * jnp.exp(-0.5 * pre * pre) * 0.3989422804014327
    )


def dot(a, b, lhs, rhs):
    return lax.dot_general(a, b, (((lhs,), (rhs,)), ((), ())), preferred_element_type=F32)


def exchange(block, axes):
    return lax.all_to_all(block, axes, 0, 0, tiled=True)


def spread(block, axes, count):
    return exchange(jnp.broadcast_to(block[None], (count,) + block.shape), axes)


def swap_core(block):
    return lax.ppermute(block, "c", [(0, 1), (1, 0)])


def from_partner(block, mask):
    if mask == 8:
        return lax.ppermute(block, "h", [(0, 1), (1, 0)])
    return lax.ppermute(block, "z", [(k, k ^ mask) for k in range(Z)])


def body(inputs, block_weights, partners, code_in, code_out, upstream):
    core = lax.axis_index("c")
    row = lax.axis_index("h") * Z + lax.axis_index("z")
    own = inputs.shape[0]
    width = block_weights.shape[2]
    rows = block_weights.shape[3]
    slots = len(MASKS)
    rank = code_in.shape[1]
    peers = X * Y
    tokens = peers * own

    targets = jnp.bitwise_xor(row, jnp.array(MASKS, jnp.int32))
    select = partners[0][None, :] == targets[:, None]
    slot_of = jnp.argmax(select, axis=1)
    kind_of = jnp.argmax(select, axis=0)

    near = spread(inputs, ("y",), Y).reshape(Y * own, rows)
    tile = spread(near, ("x",), X).reshape(tokens, rows)

    factor = code_out[:, 0, :].T
    half = width // 2
    packed = jnp.concatenate([factor[:half], factor[half:]], axis=1)
    mine = jnp.concatenate([block_weights[0].reshape(slots * width, rows), packed], axis=0)
    other = swap_core(mine)
    last = other[slots * width :]
    factor = jnp.concatenate([factor, last[:, :rank], last[:, rank:]], axis=0)
    weights = jnp.concatenate(
        [block_weights[0], other[: slots * width].reshape(slots, width, rows)], axis=1
    )
    weights = weights[slot_of]
    columns = 2 * width

    codes = dot(inputs, code_in, 1, 0)
    for mask in MASKS[1:]:
        codes = codes + from_partner(codes, mask)
    codes = codes.astype(BF16)

    sent = upstream[0].T.reshape(own, peers, columns).transpose(1, 0, 2)
    sent = jnp.concatenate(
        [sent, jnp.broadcast_to(codes[None], (peers, own, rank))], axis=2
    )
    sent = exchange(sent, ("x", "y")).reshape(tokens, columns + rank)
    slopes_in = sent[:, :columns].astype(F32)
    slopes_in = jnp.where(core == 0, slopes_in, jnp.roll(slopes_in, width, axis=1))
    codes = sent[:, columns:]

    products = dot(tile, weights.reshape(slots * columns, rows), 1, 1)
    hidden = products[:, :columns]
    for kind in (3, 4, 2, 1):
        term = products[:, kind * columns : (kind + 1) * columns].astype(BF16)
        hidden = hidden + from_partner(term, MASKS[kind]).astype(F32)
    hidden = hidden + dot(codes, factor, 1, 1)
    dpre = (slopes_in * gelu_slope(hidden)).astype(BF16)

    back = dot(dpre, factor, 1, 0).astype(BF16).reshape(peers, own, rank)
    back = exchange(back, ("x", "y")).astype(F32).sum(0).astype(BF16)
    back = spread(back, ("h", "z"), H * Z).astype(F32).sum(0)
    back = back.astype(BF16)

    kinds = [dpre] + [from_partner(dpre, mask) for mask in MASKS[1:]]
    stacked = jnp.concatenate(kinds, axis=1)

    partial = dot(stacked, weights.reshape(slots * columns, rows), 1, 0)
    partial = partial.astype(BF16).reshape(X, Y * own, rows)
    partial = exchange(partial, ("x",)).astype(F32).sum(0).astype(BF16)
    partial = exchange(partial.reshape(Y, own, rows), ("y",)).astype(F32).sum(0)
    input_grad = (partial + dot(back, code_in, 1, 1)).astype(BF16)

    block_grad = dot(stacked, tile, 0, 0).reshape(slots, columns, rows)[kind_of]
    factor_grad = dot(dpre, codes, 0, 0)
    away = factor_grad[width:]
    away = jnp.concatenate([away[:half], away[half:]], axis=1)
    away = jnp.concatenate([block_grad[:, width:].reshape(slots * width, rows), away], axis=0)
    came = swap_core(away)
    block_grad = block_grad[:, :width] + came[: slots * width].reshape(slots, width, rows)
    last = came[slots * width :]
    factor_grad = factor_grad[:width] + jnp.concatenate([last[:, :rank], last[:, rank:]], axis=0)

    back = spread(back, ("y",), Y).reshape(Y * own, rank)
    back = spread(back, ("x",), X).reshape(tokens, rank)
    code_in_grad = dot(tile, back, 0, 0)
    code_in_grad = code_in_grad + swap_core(code_in_grad)

    return (input_grad, block_grad[None], code_in_grad, factor_grad.T[:, None, :])


def solution(mesh):
    fine = Mesh(mesh.devices.reshape(X, Y, C, H, Z), ("x", "y", "c", "h", "z"))
    dp, mp = ("x", "y", "c"), ("h", "z")
    in_specs = (
        P(dp, mp),
        P(mp, None, dp, None),
        P(mp, None),
        P(mp, None),
        P(None, mp, dp),
        P(mp, None, dp),
    )
    out_specs = (P(dp, mp), P(mp, None, dp, None), P(mp, None), P(None, mp, dp))
    return jax.shard_map(body, mesh=fine, in_specs=in_specs, out_specs=out_specs, check_vma=False)
```

time: 781 us -> 210 us (0.27)
  the two profiles are of different devices: /device:TPU:64 before, /device:TPU:6 now
where the time goes in v1:
time: 210 us; the launch traced here: 206 us
  starting transfers between devices  121 us (58%)
  waiting for transfers between devices  40.1 us (19%)
  local copies, waits for them, and re-layouts  19.8 us (9%)
  matrix products  15.9 us (8%)
  other arithmetic  7.95 us (4%)
    all_to_all x9, starting transfers between devices, exchange(): return lax.all_to_all(block, axes, 0, 0, tiled=True)  55 us
    ppermute x9, starting transfers between devices, from_partner(): return lax.ppermute(block, 'z', [(k, k ^ mask) for k in range(Z)])  45.7 us
    ppermute x9, waiting for transfers between devices, from_partner(): return lax.ppermute(block, 'z', [(k, k ^ mask) for k in range(Z)])  23.3 us
    dot_general x9, matrix products, dot(): lax.dot_general(a, b, (((lhs,), (rhs,)), ((), ())), preferred_element_typ...  15.9 us
    ppermute x3, starting transfers between devices, from_partner(): return lax.ppermute(block, 'h', [(0, 1), (1, 0)])  14.9 us
    all_to_all x9, waiting for transfers between devices, exchange(): return lax.all_to_all(block, axes, 0, 0, tiled=True)  10.3 us
    unnamed x42, local copies, waits for them, and re-layouts  6.77 us
    broadcast_in_dim x6, local copies, waits for them, and re-layouts, spread(): return exchange(jnp.broadcast_to(block[None], (count,) + block.shape), axes)  6.14 us
  transfers between devices with their start and end apart: 24, of which 10 were waited for; matrix products, arithmetic and copies ran while one was open for 15% of the time, Pallas kernels for 0%

profile of v1, /device:TPU:6, one launch (start us, length us, event | category | flops | bytes accessed | tf_op | source)
XLA Modules:
  0.0 206.2 jit_solution(7192324990981804405)
XLA Ops:
  2.2 4.9 %all-to-all-start.1 = ((bf16[4,64,512]{2,1,0:T(8,128)(2,1)}), bf16[4,64,512]{2,1,0:T(8,128)(2,1)S(1)}, u32[]{:S(2)}, u32[]{:S(2)}) async-start(bf16[4,64,512]{2,1,0:T(8,128)(2,1)} %broadcast_in_dim.26), calls=%async_computation.1 | async-start | bytes 524288 | tf_op jit(solution)/shard_map/all_to_all | solution.py:24
  8.1 4.3 %collective-permute-start = (f32[64,256]{1,0:T(8,128)S(1)}, f32[64,256]{1,0:T(8,128)S(1)}, u32[]{:S(2)}, u32[]{:S(2)}) collective-permute-start(f32[64,256]{1,0:T(8,128)S(1)} %fusion.28), channel_id=1, source_target_pairs={{0,1},{1,0},{2,3},{3,2},{4,5},{5,4},{6,7},{7,6},{8,9},{9,8},{10,11... | collective-permute-start | bytes 196616 | tf_op jit(solution)/shard_map/ppermute | solution.py:38
  12.4 2.2 %collective-permute-done = f32[64,256]{1,0:T(8,128)S(1)} collective-permute-done((f32[64,256]{1,0:T(8,128)S(1)}, f32[64,256]{1,0:T(8,128)S(1)}, u32[]{:S(2)}, u32[]{:S(2)}) %collective-permute-start) | collective-permute-done | bytes 65568 | tf_op jit(solution)/shard_map/ppermute | solution.py:38
  14.7 6.1 %collective-permute-start.1 = (f32[64,256]{1,0:T(8,128)S(1)}, f32[64,256]{1,0:T(8,128)S(1)}, u32[]{:S(2)}, u32[]{:S(2)}) collective-permute-start(f32[64,256]{1,0:T(8,128)S(1)} %add.57), channel_id=1, source_target_pairs={{0,2},{1,3},{2,0},{3,1},{4,6},{5,7},{6,4},{7,5},{8,10},{9,11},{10,... | collective-permute-start | bytes 196616 | tf_op jit(solution)/shard_map/ppermute | solution.py:38
  21.9 4.9 %all-to-all-start.2 = ((bf16[4,256,512]{2,1,0:T(8,128)(2,1)}), bf16[4,256,512]{2,1,0:T(8,128)(2,1)S(1)}, u32[]{:S(2)}, u32[]{:S(2)}) async-start(bf16[4,256,512]{2,1,0:T(8,128)(2,1)} %broadcast_in_dim.55), calls=%async_computation.2 | async-start | bytes 2097152 | tf_op jit(solution)/shard_map/all_to_all | solution.py:24
  26.8 8.8 %collective-permute-start.2 = (f32[64,256]{1,0:T(8,128)S(1)}, f32[64,256]{1,0:T(8,128)S(1)}, u32[]{:S(2)}, u32[]{:S(2)}) collective-permute-start(f32[64,256]{1,0:T(8,128)S(1)} %add.58), channel_id=1, source_target_pairs={{0,4},{1,5},{2,6},{3,7},{4,0},{5,1},{6,2},{7,3},{8,12},{9,13},{10,... | collective-permute-start | bytes 196616 | tf_op jit(solution)/shard_map/ppermute | solution.py:38
  38.5 5.6 %collective-permute-start.3 = (f32[64,256]{1,0:T(8,128)S(1)}, f32[64,256]{1,0:T(8,128)S(1)}, u32[]{:S(2)}, u32[]{:S(2)}) collective-permute-start(f32[64,256]{1,0:T(8,128)S(1)} %add.59), channel_id=1, source_target_pairs={{0,8},{8,0},{1,9},{9,1},{2,10},{10,2},{3,11},{11,3},{4,12},{12,4},... | collective-permute-start | bytes 196616 | tf_op jit(solution)/shard_map/ppermute | solution.py:37
  44.3 4.3 %collective-permute-done.3 = f32[64,256]{1,0:T(8,128)S(1)} collective-permute-done((f32[64,256]{1,0:T(8,128)S(1)}, f32[64,256]{1,0:T(8,128)S(1)}, u32[]{:S(2)}, u32[]{:S(2)}) %collective-permute-start.3) | collective-permute-done | bytes 65568 | tf_op jit(solution)/shard_map/ppermute | solution.py:37
  49.7 7.9 %all-to-all-start = ((bf16[16,64,384]{2,1,0:T(8,128)(2,1)}), bf16[16,64,384]{2,1,0:T(8,128)(2,1)S(1)}, u32[]{:S(2)}, u32[]{:S(2)}) async-start(bf16[16,64,384]{2,1,0:T(8,128)(2,1)} %pad_maximum_fusion), calls=%async_computation | async-start | bytes 1572864 | tf_op jit(solution)/shard_map/all_to_all | solution.py:24
  59.8 2.4 %fusion.27 = (bf16[1024,640]{0,1:T(8,128)(2,1)S(1)}, f32[1024,640]{0,1:T(8,128)}) fusion(bf16[640,512]{1,0:T(8,128)(2,1)S(1)} %bitcast.62, bf16[1024,512]{1,0:T(8,128)(2,1)S(1)} %bitcast.55), kind=kOutput, calls=%fused_computation.56 | convolution fusion | flops 671744000 | bytes 5636096 | tf_op jit(solution)/shard_map/dot_general | solution.py:20
  63.1 4.3 %collective-permute-start.8 = (bf16[1024,128]{0,1:T(8,128)(2,1)}, bf16[1024,128]{0,1:T(8,128)(2,1)}, u32[]{:S(2)}, u32[]{:S(2)}) collective-permute-start(bf16[1024,128]{0,1:T(8,128)(2,1)} %get-tuple-element.25), channel_id=1, source_target_pairs={{0,1},{1,0},{2,3},{3,2},{4,5},{5,4},{6,7},{7,6},{8,9},{9,8},{10,11... | collective-permute-start | bytes 786440 | tf_op jit(solution)/shard_map/ppermute | solution.py:38
  69.4 6.0 %collective-permute-start.6 = (bf16[1024,128]{0,1:T(8,128)(2,1)}, bf16[1024,128]{0,1:T(8,128)(2,1)}, u32[]{:S(2)}, u32[]{:S(2)}) collective-permute-start(bf16[1024,128]{0,1:T(8,128)(2,1)} %get-tuple-element.27), channel_id=1, source_target_pairs={{0,8},{8,0},{1,9},{9,1},{2,10},{10,2},{3,11},{11,3},{4,12},{12,4},... | collective-permute-start | bytes 786440 | tf_op jit(solution)/shard_map/ppermute | solution.py:37
  75.4 7.8 %collective-permute-start.5 = (bf16[1024,128]{0,1:T(8,128)(2,1)}, bf16[1024,128]{0,1:T(8,128)(2,1)}, u32[]{:S(2)}, u32[]{:S(2)}) collective-permute-start(bf16[1024,128]{0,1:T(8,128)(2,1)} %get-tuple-element.24), channel_id=1, source_target_pairs={{0,4},{1,5},{2,6},{3,7},{4,0},{5,1},{6,2},{7,3},{8,12},{9,13},{10,... | collective-permute-start | bytes 786440 | tf_op jit(solution)/shard_map/ppermute | solution.py:38
  84.2 8.7 %collective-permute-done.5 = bf16[1024,128]{0,1:T(8,128)(2,1)} collective-permute-done((bf16[1024,128]{0,1:T(8,128)(2,1)}, bf16[1024,128]{0,1:T(8,128)(2,1)}, u32[]{:S(2)}, u32[]{:S(2)}) %collective-permute-start.5) | collective-permute-done | bytes 262176 | tf_op jit(solution)/shard_map/ppermute | solution.py:38
  92.9 2.7 %constant_dynamic-update-slice_fusion.4 = (bf16[1024,640]{0,1:T(8,128)(2,1)}, bf16[1024,128]{0,1:T(8,128)(2,1)S(1)}) fusion(bf16[32,256]{1,0:T(8,128)(2,1)S(1)} %get-tuple-element.31, bf16[32,256]{1,0:T(8,128)(2,1)S(1)} %get-tuple-element.30, bf16[64,256]{1,0:T(8,128)(2,1)S(1)} %bitcast.74, bf16[1024,384]{1,0:T(8,128)(2,1)S(1)} %bitcast.59, ...), kind=kOutput, calls=%fused_computation.40 | convolution fusion | flops 70189056 | bytes 3473409 | tf_op jit(solution)/shard_map/dot_general | solution.py:20
  96.7 7.5 %all-to-all-start.5 = ((bf16[16,64,256]{2,1,0:T(8,128)(2,1)}), bf16[16,64,256]{2,1,0:T(8,128)(2,1)S(1)}, u32[]{:S(2)}, u32[]{:S(2)}) async-start(bf16[16,64,256]{2,1,0:T(8,128)(2,1)} %bitcast.64), calls=%async_computation.5 | async-start | bytes 1048576 | tf_op jit(solution)/shard_map/all_to_all | solution.py:24
  104.8 4.4 %collective-permute-start.9 = (bf16[1024,128]{0,1:T(8,128)(2,1)}, bf16[1024,128]{0,1:T(8,128)(2,1)}, u32[]{:S(2)}, u32[]{:S(2)}) collective-permute-start(bf16[1024,128]{0,1:T(8,128)(2,1)} %copy-done.4), channel_id=1, source_target_pairs={{0,1},{1,0},{2,3},{3,2},{4,5},{5,4},{6,7},{7,6},{8,9},{9,8},{10,11... | collective-permute-start | bytes 786440 | tf_op jit(solution)/shard_map/ppermute | solution.py:38
  111.2 6.1 %collective-permute-start.11 = (bf16[1024,128]{0,1:T(8,128)(2,1)}, bf16[1024,128]{0,1:T(8,128)(2,1)}, u32[]{:S(2)}, u32[]{:S(2)}) collective-permute-start(bf16[1024,128]{0,1:T(8,128)(2,1)} %copy-done.4), channel_id=1, source_target_pairs={{0,4},{1,5},{2,6},{3,7},{4,0},{5,1},{6,2},{7,3},{8,12},{9,13},{10,... | collective-permute-start | bytes 786440 | tf_op jit(solution)/shard_map/ppermute | solution.py:38
  117.3 3.3 %collective-permute-start.12 = (bf16[1024,128]{0,1:T(8,128)(2,1)}, bf16[1024,128]{0,1:T(8,128)(2,1)}, u32[]{:S(2)}, u32[]{:S(2)}) collective-permute-start(bf16[1024,128]{0,1:T(8,128)(2,1)} %copy-done.4), channel_id=1, source_target_pairs={{0,8},{8,0},{1,9},{9,1},{2,10},{10,2},{3,11},{11,3},{4,12},{12,4},... | collective-permute-start | bytes 786440 | tf_op jit(solution)/shard_map/ppermute | solution.py:37
  122.7 8.1 %all-to-all-start.6 = ((bf16[16,64,256]{2,1,0:T(8,128)(2,1)}), bf16[16,64,256]{2,1,0:T(8,128)(2,1)}, u32[]{:S(2)}, u32[]{:S(2)}) async-start(bf16[16,64,256]{2,1,0:T(8,128)(2,1)} %broadcast_in_dim.56), calls=%async_computation.6 | async-start | bytes 1048576 | tf_op jit(solution)/shard_map/all_to_all | solution.py:24
  132.5 11.4 %collective-permute-done.10 = bf16[1024,128]{0,1:T(8,128)(2,1)} collective-permute-done((bf16[1024,128]{0,1:T(8,128)(2,1)}, bf16[1024,128]{0,1:T(8,128)(2,1)}, u32[]{:S(2)}, u32[]{:S(2)}) %collective-permute-start.10) | collective-permute-done | bytes 262176 | tf_op jit(solution)/shard_map/ppermute | solution.py:38
  154.0 7.2 %all-to-all-start.7 = ((bf16[4,64,256]{2,1,0:T(8,128)(2,1)}), bf16[4,64,256]{2,1,0:T(8,128)(2,1)S(1)}, u32[]{:S(2)}, u32[]{:S(2)}) async-start(bf16[4,64,256]{2,1,0:T(8,128)(2,1)} %broadcast_in_dim.59), calls=%async_computation.7 | async-start | bytes 262144 | tf_op jit(solution)/shard_map/all_to_all | solution.py:24
  161.2 3.3 %convolution_convert_fusion = bf16[1024,512]{1,0:T(8,128)(2,1)} fusion(bf16[1024,640]{0,1:T(8,128)(2,1)} %copy-done.16, bf16[640,512]{1,0:T(8,128)(2,1)S(1)} %bitcast.63), kind=kOutput, calls=%fused_computation.3 | convolution fusion | flops 671612928 | bytes 3014656 | tf_op jit(solution)/shard_map/dot_general | solution.py:20
  164.5 2.6 %all-to-all-done.7 = bf16[4,64,256]{2,1,0:T(8,128)(2,1)S(1)} async-done(((bf16[4,64,256]{2,1,0:T(8,128)(2,1)}), bf16[4,64,256]{2,1,0:T(8,128)(2,1)S(1)}, u32[]{:S(2)}, u32[]{:S(2)}) %all-to-all-start.7) | async-done | bytes 131104 | tf_op jit(solution)/shard_map/all_to_all | solution.py:24
  167.1 4.9 %all-to-all-start.3 = ((bf16[4,256,512]{2,1,0:T(8,128)(2,1)}), bf16[4,256,512]{2,1,0:T(8,128)(2,1)}, u32[]{:S(2)}, u32[]{:S(2)}) async-start(bf16[4,256,512]{2,1,0:T(8,128)(2,1)} %bitcast.69), calls=%async_computation.3 | async-start | bytes 2097152 | tf_op jit(solution)/shard_map/all_to_all | solution.py:24
  174.0 2.2 %collective-permute-done.13 = f32[352,512]{1,0:T(8,128)S(1)} collective-permute-done((f32[352,512]{1,0:T(8,128)S(1)}, f32[352,512]{1,0:T(8,128)S(1)}, u32[]{:S(2)}, u32[]{:S(2)}) %collective-permute-start.13) | collective-permute-done | bytes 720928 | tf_op jit(solution)/shard_map/ppermute | solution.py:32
  178.2 2.7 %all-to-all-done.3 = bf16[4,256,512]{2,1,0:T(8,128)(2,1)} async-done(((bf16[4,256,512]{2,1,0:T(8,128)(2,1)}), bf16[4,256,512]{2,1,0:T(8,128)(2,1)}, u32[]{:S(2)}, u32[]{:S(2)}) %all-to-all-start.3) | async-done | bytes 1048608 | tf_op jit(solution)/shard_map/all_to_all | solution.py:24
  181.8 6.2 %all-to-all-start.8 = ((bf16[4,256,256]{1,2,0:T(8,128)(2,1)}), bf16[4,256,256]{1,2,0:T(8,128)(2,1)}, u32[]{:S(2)}, u32[]{:S(2)}) async-start(bf16[4,256,256]{1,2,0:T(8,128)(2,1)} %broadcast_in_dim.61), calls=%async_computation.8 | async-start | bytes 1048576 | tf_op jit(solution)/shard_map/all_to_all | solution.py:24
  189.7 2.1 %reduce_sum.45 = bf16[256,512]{1,0:T(8,128)(2,1)} reduce(bf16[4,256,512]{2,1,0:T(8,128)(2,1)} %all-to-all-done.3, bf16[]{:T(256)} %constant.45.clone.1), dimensions={0}, to_apply=%region_1.2 | reduce | flops 393216 | bytes 1310722 | tf_op jit(solution)/shard_map/reduce_sum | solution.py:105
  191.8 2.2 %all-to-all-done.8 = bf16[4,256,256]{1,2,0:T(8,128)(2,1)} async-done(((bf16[4,256,256]{1,2,0:T(8,128)(2,1)}), bf16[4,256,256]{1,2,0:T(8,128)(2,1)}, u32[]{:S(2)}, u32[]{:S(2)}) %all-to-all-start.8) | async-done | bytes 524320 | tf_op jit(solution)/shard_map/all_to_all | solution.py:24
  194.1 3.4 %all-to-all-start.4 = ((bf16[4,64,512]{2,1,0:T(8,128)(2,1)}), bf16[4,64,512]{2,1,0:T(8,128)(2,1)S(1)}, u32[]{:S(2)}, u32[]{:S(2)}) async-start(bf16[4,64,512]{2,1,0:T(8,128)(2,1)} %bitcast.16), calls=%async_computation.4 | async-start | bytes 524288 | tf_op jit(solution)/shard_map/all_to_all | solution.py:24
  201.6 2.7 %all-to-all-done.4 = bf16[4,64,512]{2,1,0:T(8,128)(2,1)S(1)} async-done(((bf16[4,64,512]{2,1,0:T(8,128)(2,1)}), bf16[4,64,512]{2,1,0:T(8,128)(2,1)S(1)}, u32[]{:S(2)}, u32[]{:S(2)}) %all-to-all-start.4) | async-done | bytes 262176 | tf_op jit(solution)/shard_map/all_to_all | solution.py:24
  (111 shorter events, 43.8 us)
Async XLA Ops:
  2.2 18.5 %all-to-all-start.1 = ((bf16[4,64,512]{2,1,0:T(8,128)(2,1)}), bf16[4,64,512]{2,1,0:T(8,128)(2,1)S(1)}, u32[]{:S(2)}, u32[]{:S(2)}) async-start(bf16[4,64,512]{2,1,0:T(8,128)(2,1)} %broadcast_in_dim.26), calls=%async_computation.1 | async-start | bytes 524288 | tf_op jit(solution)/shard_map/all_to_all | solution.py:24
  8.1 6.5 %collective-permute-start = (f32[64,256]{1,0:T(8,128)S(1)}, f32[64,256]{1,0:T(8,128)S(1)}, u32[]{:S(2)}, u32[]{:S(2)}) collective-permute-start(f32[64,256]{1,0:T(8,128)S(1)} %fusion.28), channel_id=1, source_target_pairs={{0,1},{1,0},{2,3},{3,2},{4,5},{5,4},{6,7},{7,6},{8,9},{9,8},{10,11... | collective-permute-start | bytes 196616 | tf_op jit(solution)/shard_map/ppermute | solution.py:38
  14.7 12.1 %collective-permute-start.1 = (f32[64,256]{1,0:T(8,128)S(1)}, f32[64,256]{1,0:T(8,128)S(1)}, u32[]{:S(2)}, u32[]{:S(2)}) collective-permute-start(f32[64,256]{1,0:T(8,128)S(1)} %add.57), channel_id=1, source_target_pairs={{0,2},{1,3},{2,0},{3,1},{4,6},{5,7},{6,4},{7,5},{8,10},{9,11},{10,... | collective-permute-start | bytes 196616 | tf_op jit(solution)/shard_map/ppermute | solution.py:38
  21.9 13.7 %copy-start.3 = (bf16[1,5,64,512]{3,2,1,0:T(8,128)(2,1)S(1)}, bf16[1,5,64,512]{3,2,1,0:T(8,128)(2,1)}, u32[]{:S(2)}) copy-start(bf16[1,5,64,512]{3,2,1,0:T(8,128)(2,1)} %param.8) | copy-start | bytes 983044
  21.9 22.3 %copy-start.17 = (s32[5]{0:T(128)S(1)}, s32[5]{0:T(128)}, u32[]{:S(2)}) copy-start(s32[5]{0:T(128)} %constant.47.clone) | copy-start | bytes 64
  21.9 22.3 %copy-start.10 = (bf16[1,2048,64]{1,2,0:T(8,128)(2,1)S(1)}, bf16[1,2048,64]{1,2,0:T(8,128)(2,1)}, u32[]{:S(2)}) copy-start(bf16[1,2048,64]{1,2,0:T(8,128)(2,1)} %param.12) | copy-start | bytes 786436
  21.9 27.8 %all-to-all-start.2 = ((bf16[4,256,512]{2,1,0:T(8,128)(2,1)}), bf16[4,256,512]{2,1,0:T(8,128)(2,1)S(1)}, u32[]{:S(2)}, u32[]{:S(2)}) async-start(bf16[4,256,512]{2,1,0:T(8,128)(2,1)} %broadcast_in_dim.55), calls=%async_computation.2 | async-start | bytes 2097152 | tf_op jit(solution)/shard_map/all_to_all | solution.py:24
  26.8 11.7 %collective-permute-start.2 = (f32[64,256]{1,0:T(8,128)S(1)}, f32[64,256]{1,0:T(8,128)S(1)}, u32[]{:S(2)}, u32[]{:S(2)}) collective-permute-start(f32[64,256]{1,0:T(8,128)S(1)} %add.58), channel_id=1, source_target_pairs={{0,4},{1,5},{2,6},{3,7},{4,0},{5,1},{6,2},{7,3},{8,12},{9,13},{10,... | collective-permute-start | bytes 196616 | tf_op jit(solution)/shard_map/ppermute | solution.py:38
  35.6 22.7 %collective-permute-start.4 = (bf16[352,512]{1,0:T(8,128)(2,1)S(1)}, bf16[352,512]{1,0:T(8,128)(2,1)S(1)}, u32[]{:S(2)}, u32[]{:S(2)}) collective-permute-start(bf16[352,512]{1,0:T(8,128)(2,1)S(1)} %maximum_maximum_fusion.1), channel_id=1, source_target_pairs={{0,16},{16,0},{1,17},{17,1},{2,18},{18,2},{3,19},{19,3},{4,20},{20... | collective-permute-start | bytes 1081352 | tf_op jit(solution)/shard_map/ppermute | solution.py:32
  38.5 10.1 %collective-permute-start.3 = (f32[64,256]{1,0:T(8,128)S(1)}, f32[64,256]{1,0:T(8,128)S(1)}, u32[]{:S(2)}, u32[]{:S(2)}) collective-permute-start(f32[64,256]{1,0:T(8,128)S(1)} %add.59), channel_id=1, source_target_pairs={{0,8},{8,0},{1,9},{9,1},{2,10},{10,2},{3,11},{11,3},{4,12},{12,4},... | collective-permute-start | bytes 196616 | tf_op jit(solution)/shard_map/ppermute | solution.py:37
  48.7 9.0 %copy-start.14 = (s32[1,5]{1,0:T(1,128)S(1)}, s32[1,5]{1,0:T(1,128)}, u32[]{:S(2)}) copy-start(s32[1,5]{1,0:T(1,128)} %param.9) | copy-start | bytes 64
  49.7 34.2 %all-to-all-start = ((bf16[16,64,384]{2,1,0:T(8,128)(2,1)}), bf16[16,64,384]{2,1,0:T(8,128)(2,1)S(1)}, u32[]{:S(2)}, u32[]{:S(2)}) async-start(bf16[16,64,384]{2,1,0:T(8,128)(2,1)} %pad_maximum_fusion), calls=%async_computation | async-start | bytes 1572864 | tf_op jit(solution)/shard_map/all_to_all | solution.py:24
  63.1 21.0 %collective-permute-start.8 = (bf16[1024,128]{0,1:T(8,128)(2,1)}, bf16[1024,128]{0,1:T(8,128)(2,1)}, u32[]{:S(2)}, u32[]{:S(2)}) collective-permute-start(bf16[1024,128]{0,1:T(8,128)(2,1)} %get-tuple-element.25), channel_id=1, source_target_pairs={{0,1},{1,0},{2,3},{3,2},{4,5},{5,4},{6,7},{7,6},{8,9},{9,8},{10,11... | collective-permute-start | bytes 786440 | tf_op jit(solution)/shard_map/ppermute | solution.py:38
  67.4 16.8 %collective-permute-start.7 = (bf16[1024,128]{0,1:T(8,128)(2,1)}, bf16[1024,128]{0,1:T(8,128)(2,1)}, u32[]{:S(2)}, u32[]{:S(2)}) collective-permute-start(bf16[1024,128]{0,1:T(8,128)(2,1)} %get-tuple-element.26), channel_id=1, source_target_pairs={{0,2},{1,3},{2,0},{3,1},{4,6},{5,7},{6,4},{7,5},{8,10},{9,11},{10,... | collective-permute-start | bytes 786440 | tf_op jit(solution)/shard_map/ppermute | solution.py:38
  69.4 14.9 %collective-permute-start.6 = (bf16[1024,128]{0,1:T(8,128)(2,1)}, bf16[1024,128]{0,1:T(8,128)(2,1)}, u32[]{:S(2)}, u32[]{:S(2)}) collective-permute-start(bf16[1024,128]{0,1:T(8,128)(2,1)} %get-tuple-element.27), channel_id=1, source_target_pairs={{0,8},{8,0},{1,9},{9,1},{2,10},{10,2},{3,11},{11,3},{4,12},{12,4},... | collective-permute-start | bytes 786440 | tf_op jit(solution)/shard_map/ppermute | solution.py:37
  75.4 17.6 %collective-permute-start.5 = (bf16[1024,128]{0,1:T(8,128)(2,1)}, bf16[1024,128]{0,1:T(8,128)(2,1)}, u32[]{:S(2)}, u32[]{:S(2)}) collective-permute-start(bf16[1024,128]{0,1:T(8,128)(2,1)} %get-tuple-element.24), channel_id=1, source_target_pairs={{0,4},{1,5},{2,6},{3,7},{4,0},{5,1},{6,2},{7,3},{8,12},{9,13},{10,... | collective-permute-start | bytes 786440 | tf_op jit(solution)/shard_map/ppermute | solution.py:38
  96.7 25.1 %all-to-all-start.5 = ((bf16[16,64,256]{2,1,0:T(8,128)(2,1)}), bf16[16,64,256]{2,1,0:T(8,128)(2,1)S(1)}, u32[]{:S(2)}, u32[]{:S(2)}) async-start(bf16[16,64,256]{2,1,0:T(8,128)(2,1)} %bitcast.64), calls=%async_computation.5 | async-start | bytes 1048576 | tf_op jit(solution)/shard_map/all_to_all | solution.py:24
  104.8 26.7 %collective-permute-start.9 = (bf16[1024,128]{0,1:T(8,128)(2,1)}, bf16[1024,128]{0,1:T(8,128)(2,1)}, u32[]{:S(2)}, u32[]{:S(2)}) collective-permute-start(bf16[1024,128]{0,1:T(8,128)(2,1)} %copy-done.4), channel_id=1, source_target_pairs={{0,1},{1,0},{2,3},{3,2},{4,5},{5,4},{6,7},{7,6},{8,9},{9,8},{10,11... | collective-permute-start | bytes 786440 | tf_op jit(solution)/shard_map/ppermute | solution.py:38
  109.2 34.7 %collective-permute-start.10 = (bf16[1024,128]{0,1:T(8,128)(2,1)}, bf16[1024,128]{0,1:T(8,128)(2,1)}, u32[]{:S(2)}, u32[]{:S(2)}) collective-permute-start(bf16[1024,128]{0,1:T(8,128)(2,1)} %copy-done.4), channel_id=1, source_target_pairs={{0,2},{1,3},{2,0},{3,1},{4,6},{5,7},{6,4},{7,5},{8,10},{9,11},{10,... | collective-permute-start | bytes 786440 | tf_op jit(solution)/shard_map/ppermute | solution.py:38
  111.2 33.7 %collective-permute-start.11 = (bf16[1024,128]{0,1:T(8,128)(2,1)}, bf16[1024,128]{0,1:T(8,128)(2,1)}, u32[]{:S(2)}, u32[]{:S(2)}) collective-permute-start(bf16[1024,128]{0,1:T(8,128)(2,1)} %copy-done.4), channel_id=1, source_target_pairs={{0,4},{1,5},{2,6},{3,7},{4,0},{5,1},{6,2},{7,3},{8,12},{9,13},{10,... | collective-permute-start | bytes 786440 | tf_op jit(solution)/shard_map/ppermute | solution.py:38
  117.3 28.6 %collective-permute-start.12 = (bf16[1024,128]{0,1:T(8,128)(2,1)}, bf16[1024,128]{0,1:T(8,128)(2,1)}, u32[]{:S(2)}, u32[]{:S(2)}) collective-permute-start(bf16[1024,128]{0,1:T(8,128)(2,1)} %copy-done.4), channel_id=1, source_target_pairs={{0,8},{8,0},{1,9},{9,1},{2,10},{10,2},{3,11},{11,3},{4,12},{12,4},... | collective-permute-start | bytes 786440 | tf_op jit(solution)/shard_map/ppermute | solution.py:37
  121.9 9.6 %copy-start.15 = (bf16[1024,640]{0,1:T(8,128)(2,1)S(1)}, bf16[1024,640]{0,1:T(8,128)(2,1)}, u32[]{:S(2)}) copy-start(bf16[1024,640]{0,1:T(8,128)(2,1)} %get-tuple-element.40) | copy-start | bytes 3932164
  122.7 29.0 %all-to-all-start.6 = ((bf16[16,64,256]{2,1,0:T(8,128)(2,1)}), bf16[16,64,256]{2,1,0:T(8,128)(2,1)}, u32[]{:S(2)}, u32[]{:S(2)}) async-start(bf16[16,64,256]{2,1,0:T(8,128)(2,1)} %broadcast_in_dim.56), calls=%async_computation.6 | async-start | bytes 1048576 | tf_op jit(solution)/shard_map/all_to_all | solution.py:24
  151.8 12.7 %copy-start.1 = (f32[5,128,512]{2,1,0:T(8,128)}, f32[5,128,512]{2,1,0:T(8,128)S(1)}, u32[]{:S(2)}) copy-start(f32[5,128,512]{2,1,0:T(8,128)S(1)} %gather_fusion.1) | copy-start | bytes 3932164
  154.0 13.1 %all-to-all-start.7 = ((bf16[4,64,256]{2,1,0:T(8,128)(2,1)}), bf16[4,64,256]{2,1,0:T(8,128)(2,1)S(1)}, u32[]{:S(2)}, u32[]{:S(2)}) async-start(bf16[4,64,256]{2,1,0:T(8,128)(2,1)} %broadcast_in_dim.59), calls=%async_computation.7 | async-start | bytes 262144 | tf_op jit(solution)/shard_map/all_to_all | solution.py:24
  164.5 7.5 %copy-start.12 = (f32[32,256]{1,0:T(8,128)S(1)}, f32[32,256]{1,0:T(8,128)}, u32[]{:S(2)}) copy-start(f32[32,256]{1,0:T(8,128)} %get-tuple-element.35) | copy-start | bytes 98308
  167.1 13.9 %all-to-all-start.3 = ((bf16[4,256,512]{2,1,0:T(8,128)(2,1)}), bf16[4,256,512]{2,1,0:T(8,128)(2,1)}, u32[]{:S(2)}, u32[]{:S(2)}) async-start(bf16[4,256,512]{2,1,0:T(8,128)(2,1)} %bitcast.69), calls=%async_computation.3 | async-start | bytes 2097152 | tf_op jit(solution)/shard_map/all_to_all | solution.py:24
  172.1 4.1 %collective-permute-start.13 = (f32[352,512]{1,0:T(8,128)S(1)}, f32[352,512]{1,0:T(8,128)S(1)}, u32[]{:S(2)}, u32[]{:S(2)}) collective-permute-start(f32[352,512]{1,0:T(8,128)S(1)} %maximum_maximum_fusion), channel_id=1, source_target_pairs={{0,16},{16,0},{1,17},{17,1},{2,18},{18,2},{3,19},{19,3},{4,20},{20... | collective-permute-start | bytes 2162696 | tf_op jit(solution)/shard_map/ppermute | solution.py:32
  177.1 11.6 %copy-start.2 = (f32[5,128,512]{2,1,0:T(8,128)S(1)}, f32[5,128,512]{2,1,0:T(8,128)}, u32[]{:S(2)}) copy-start(f32[5,128,512]{2,1,0:T(8,128)} %copy-done.1) | copy-start | bytes 3932164
  181.8 12.3 %all-to-all-start.8 = ((bf16[4,256,256]{1,2,0:T(8,128)(2,1)}), bf16[4,256,256]{1,2,0:T(8,128)(2,1)}, u32[]{:S(2)}, u32[]{:S(2)}) async-start(bf16[4,256,256]{1,2,0:T(8,128)(2,1)} %broadcast_in_dim.61), calls=%async_computation.8 | async-start | bytes 1048576 | tf_op jit(solution)/shard_map/all_to_all | solution.py:24
  194.1 10.2 %all-to-all-start.4 = ((bf16[4,64,512]{2,1,0:T(8,128)(2,1)}), bf16[4,64,512]{2,1,0:T(8,128)(2,1)S(1)}, u32[]{:S(2)}, u32[]{:S(2)}) async-start(bf16[4,64,512]{2,1,0:T(8,128)(2,1)} %bitcast.16), calls=%async_computation.4 | async-start | bytes 524288 | tf_op jit(solution)/shard_map/all_to_all | solution.py:24
  199.0 6.1 %collective-permute-start.14 = (f32[512,256]{0,1:T(8,128)S(1)}, f32[512,256]{0,1:T(8,128)S(1)}, u32[]{:S(2)}, u32[]{:S(2)}) collective-permute-start(f32[512,256]{0,1:T(8,128)S(1)} %convolution_bitcast_fusion.1), channel_id=1, source_target_pairs={{0,16},{16,0},{1,17},{17,1},{2,18},{18,2},{3,19},{19,3},{4,20},{20... | collective-permute-start | bytes 1572872 | tf_op jit(solution)/shard_map/ppermute | solution.py:32
  (11 other events, 40.2 us)

commit v2 on v1

v2 whole, which is shorter than its diff:
```python
import jax
import jax.numpy as jnp
from jax import lax
from jax.experimental import pallas as pl
from jax.experimental.pallas import tpu as pltpu
from jax.sharding import Mesh, PartitionSpec as P

F32 = jnp.float32
BF16 = jnp.bfloat16
X, Y, C, H, Z = 4, 4, 2, 2, 8
MASKS = (0, 1, 2, 4, 8)
SLOTS = 5
OWN = 64
ROWS = 512
RANK = 256
PEERS = X * Y
TOKENS = PEERS * OWN
COLS = 2 * OWN
STEP = 256


def gelu_slope(pre):
    return (
        0.5 * (1.0 + lax.erf(pre * 0.7071067811865476))
        + pre * jnp.exp(-0.5 * pre * pre) * 0.3989422804014327
    )


def dot(a, b, lhs, rhs):
    return lax.dot_general(a, b, (((lhs,), (rhs,)), ((), ())), preferred_element_type=F32)


def exchange(block, axes):
    return lax.all_to_all(block, axes, 0, 0, tiled=True)


def spread(block, axes, count):
    return exchange(jnp.broadcast_to(block[None], (count,) + block.shape), axes)


def swap_core(block):
    return lax.ppermute(block, "c", [(0, 1), (1, 0)])


def from_partner(block, mask):
    if mask == 8:
        return lax.ppermute(block, "h", [(0, 1), (1, 0)])
    return lax.ppermute(block, "z", [(k, k ^ mask) for k in range(Z)])


def after(value, *others):
    return lax.optimization_barrier((value, *others))[0]


SMEM = pl.BlockSpec(memory_space=pltpu.SMEM)
VMEM = pl.BlockSpec(memory_space=pltpu.VMEM)


def call(kernel, ins, outs, flops, *args):
    size = sum(a.size * a.dtype.itemsize for a in args)
    size += sum(int(jnp.dtype(o.dtype).itemsize) * o.size for o in outs)
    return pl.pallas_call(
        kernel,
        out_shape=outs,
        in_specs=ins,
        out_specs=[VMEM] * len(outs),
        cost_estimate=pl.CostEstimate(flops=flops, bytes_accessed=size, transcendentals=0),
        compiler_params=pltpu.CompilerParams(vmem_limit_bytes=10 * 1024 * 1024),
    )(*args)


def shape(dims, dtype):
    return jax.ShapeDtypeStruct(dims, dtype)


def all_weights(slot_ref, mine_ref, other_ref):
    parts = []
    for kind in range(SLOTS):
        slot = slot_ref[kind]
        parts.append(mine_ref[slot])
        parts.append(other_ref[pl.ds(pl.multiple_of(slot * OWN, OWN), OWN), :])
    return jnp.concatenate(parts, axis=0)


def all_factor(factor_ref, other_ref):
    last = other_ref[SLOTS * OWN :, :]
    return jnp.concatenate([factor_ref[...], last[:, :RANK], last[:, RANK:]], axis=0)


def forward_kernel(slot_ref, tile_ref, mine_ref, other_ref, *outs):
    weights = all_weights(slot_ref, mine_ref, other_ref)
    for part in range(X):
        rows = pl.ds(part * STEP, STEP)
        products = dot(tile_ref[rows, :], weights, 1, 1)
        outs[0][rows, :] = products[:, :COLS]
        for kind in range(1, SLOTS):
            outs[kind][rows, :] = products[:, kind * COLS : (kind + 1) * COLS].astype(BF16)


def hidden_kernel(core_ref, hidden_ref, a, b, c, d, sent_ref, factor_ref, other_ref, dpre_ref, back_ref):
    factor = all_factor(factor_ref, other_ref)
    core = core_ref[0]
    for part in range(X):
        rows = pl.ds(part * STEP, STEP)
        hidden = hidden_ref[rows, :]
        for arrived in (a, b, c, d):
            hidden = hidden + arrived[rows, :].astype(F32)
        hidden = hidden + dot(sent_ref[rows, COLS:], factor, 1, 1)
        up = sent_ref[rows, :COLS].astype(F32)
        up = jnp.where(core == 0, up, pltpu.roll(up, OWN, 1))
        dpre = (up * gelu_slope(hidden)).astype(BF16)
        dpre_ref[rows, :] = dpre
        back_ref[rows, :] = dot(dpre, factor, 1, 0).astype(BF16)


def input_kernel(slot_ref, a, b, c, d, e, mine_ref, other_ref, out_ref):
    weights = all_weights(slot_ref, mine_ref, other_ref)
    for part in range(X):
        rows = pl.ds(part * STEP, STEP)
        stacked = jnp.concatenate([k[rows, :] for k in (a, b, c, d, e)], axis=1)
        out_ref[rows, :] = dot(stacked, weights, 1, 0).astype(BF16)


def weight_kernel(slot_ref, a, b, c, d, e, tile_ref, sent_ref, keep_ref, away_ref, factor_ref):
    for kind, grads in enumerate((a, b, c, d, e)):
        slot = slot_ref[kind]
        full = dot(grads[...], tile_ref[...], 0, 0)
        keep_ref[slot] = full[:OWN]
        away_ref[pl.ds(pl.multiple_of(slot * OWN, OWN), OWN), :] = full[OWN:]
    full = dot(a[...], sent_ref[:, COLS:], 0, 0)
    factor_ref[...] = full[:OWN]
    away_ref[SLOTS * OWN :, :RANK] = full[OWN : OWN + OWN // 2]
    away_ref[SLOTS * OWN :, RANK:] = full[OWN + OWN // 2 :]


def code_kernel(tile_ref, back_ref, out_ref):
    out_ref[...] = dot(tile_ref[...], back_ref[...], 0, 0)


def body(inputs, block_weights, partners, code_in, code_out, upstream):
    core = lax.axis_index("c").reshape(1)
    row = lax.axis_index("h") * Z + lax.axis_index("z")

    targets = jnp.bitwise_xor(row, jnp.array(MASKS, jnp.int32))
    slots = jnp.sum(
        jnp.where(partners[0][None, :] == targets[:, None], jnp.arange(SLOTS)[None, :], 0), axis=1
    ).astype(jnp.int32)

    tile = spread(inputs, ("x", "y"), PEERS).reshape(TOKENS, ROWS)

    factor = code_out[:, 0, :].T
    packed = jnp.concatenate([factor[: OWN // 2], factor[OWN // 2 :]], axis=1)
    mine = block_weights[0]
    other = swap_core(jnp.concatenate([mine.reshape(SLOTS * OWN, ROWS), packed], axis=0))

    codes = dot(inputs, code_in, 1, 0)
    for mask in (1, 2):
        codes = codes + from_partner(codes, mask)
    codes = after(codes, other)
    codes = codes + from_partner(codes, 4)

    tall = [shape((TOKENS, COLS), BF16)] * 4
    hidden, *terms = call(
        forward_kernel, [SMEM] + [VMEM] * 3, [shape((TOKENS, COLS), F32)] + tall,
        2 * TOKENS * COLS * SLOTS * ROWS, slots, tile, mine, other,
    )
    codes = after(codes, hidden)
    codes = (codes + from_partner(codes, 8)).astype(BF16)
    arrived = [from_partner(term, mask) for term, mask in zip(terms, MASKS[1:])]

    sent = upstream[0].T.reshape(OWN, PEERS, COLS).transpose(1, 0, 2)
    sent = jnp.concatenate([sent, jnp.broadcast_to(codes[None], (PEERS, OWN, RANK))], axis=2)
    sent = exchange(sent, ("x", "y")).reshape(TOKENS, COLS + RANK)
    dpre, back = call(
        hidden_kernel, [SMEM] + [VMEM] * 8,
        [shape((TOKENS, COLS), BF16), shape((TOKENS, RANK), BF16)],
        4 * TOKENS * COLS * RANK, core, hidden, *arrived, sent, factor, other,
    )
    kinds = [dpre] + [from_partner(dpre, mask) for mask in MASKS[1:]]

    back = exchange(back.reshape(PEERS * H, OWN // H, RANK), ("x", "y", "h")).astype(F32).sum(0)

    (partial,) = call(
        input_kernel, [SMEM] + [VMEM] * 7, [shape((TOKENS, ROWS), BF16)],
        2 * TOKENS * COLS * SLOTS * ROWS, slots, *kinds, mine, other,
    )
    back = after(back, partial)
    partial = exchange(partial.reshape(X, Y * OWN, ROWS), ("x",)).astype(F32).sum(0).astype(BF16)
    for mask in MASKS[1:4]:
        back = back + from_partner(back, mask)
    back = spread(back.astype(BF16), ("x", "y", "h"), PEERS * H).reshape(TOKENS, RANK)
    partial = after(partial, back)
    partial = exchange(partial.reshape(Y, OWN, ROWS), ("y",))
    place = (lax.axis_index("x") * Y + lax.axis_index("y")) * OWN
    own_back = lax.dynamic_slice_in_dim(back, place, OWN, 0)
    input_grad = partial.astype(F32).sum(0) + dot(own_back, code_in, 1, 1)
    input_grad = input_grad.astype(BF16)

    keep, away, factor_grad = call(
        weight_kernel, [SMEM] + [VMEM] * 7,
        [shape((SLOTS, OWN, ROWS), F32), shape((SLOTS * OWN + OWN // 2, ROWS), F32), shape((OWN, RANK), F32)],
        2 * TOKENS * COLS * (SLOTS * ROWS + RANK), slots, *kinds, tile, sent,
    )
    came = swap_core(away)
    block_grad = keep + came[: SLOTS * OWN].reshape(SLOTS, OWN, ROWS)
    last = came[SLOTS * OWN :]
    factor_grad = factor_grad + jnp.concatenate([last[:, :RANK], last[:, RANK:]], axis=0)

    (code_in_grad,) = call(
        code_kernel, [VMEM] * 2, [shape((ROWS, RANK), F32)], 2 * TOKENS * ROWS * RANK, tile, back
    )
    code_in_grad = code_in_grad + swap_core(code_in_grad)

    return (input_grad, block_grad[None], code_in_grad, factor_grad.T[:, None, :])


def solution(mesh):
    fine = Mesh(mesh.devices.reshape(X, Y, C, H, Z), ("x", "y", "c", "h", "z"))
    dp, mp = ("x", "y", "c"), ("h", "z")
    in_specs = (
        P(dp, mp),
        P(mp, None, dp, None),
        P(mp, None),
        P(mp, None),
        P(None, mp, dp),
        P(mp, None, dp),
    )
    out_specs = (P(dp, mp), P(mp, None, dp, None), P(mp, None), P(None, mp, dp))
    return jax.shard_map(body, mesh=fine, in_specs=in_specs, out_specs=out_specs, check_vma=False)
```

time: 210 us -> 209 us (level); the launches traced: 206 us -> 208 us
  waiting for transfers between devices: 40.1 us -> 61.8 us
  matrix products: 15.9 us -> 1.01 us
  Pallas kernels: 0 us -> 8.73 us
  starting transfers between devices: 121 us -> 114 us
  local copies, waits for them, and re-layouts: 19.8 us -> 13.8 us
    ppermute x9 -> x12, waiting for transfers between devices: 23.3 us -> 40.4 us  [from_partner(): return lax.ppermute(block, 'z', [(k, k ^ mask) for k in range(Z)])]
    all_to_all x9 -> x6, starting transfers between devices: 55 us -> 38.9 us  [exchange(): return lax.all_to_all(block, axes, 0, 0, tiled=True)]
    dot_general x9 -> x2, matrix products: 15.9 us -> 1.01 us  [dot(): lax.dot_general(a, b, (((lhs,), (rhs,)), ((), ())), preferred_element_typ...]
    ppermute x3, waiting for transfers between devices: 4.34 us -> 13.5 us  [from_partner(): return lax.ppermute(block, 'h', [(0, 1), (1, 0)])]
    pallas_call x0 -> x5, Pallas kernels: none -> 8.73 us  [call(): pl.pallas_call(kernel, out_shape=outs, in_specs=ins, out_specs=[VMEM] * l...]
    ppermute x9 -> x12, starting transfers between devices: 45.7 us -> 51.2 us  [from_partner(): return lax.ppermute(block, 'z', [(k, k ^ mask) for k in range(Z)])]
    all_to_all x9 -> x6, waiting for transfers between devices: 10.3 us -> 5.47 us  [exchange(): return lax.all_to_all(block, axes, 0, 0, tiled=True)]
    broadcast_in_dim x6 -> x2, local copies, waits for them, and re-layouts: 6.14 us -> 2.83 us  [spread(): return exchange(jnp.broadcast_to(block[None], (count,) + block.shape), axes)]
  transfers between devices with their start and end apart: 24 -> 24, of which waited for: 10 -> 16; matrix products, arithmetic and copies ran while one was open for 15% -> 3% of each run, Pallas kernels for 0% -> 3%
where the time goes in v2:
time: 209 us; the launch traced here: 208 us
  starting transfers between devices  114 us (55%)
  waiting for transfers between devices  61.8 us (30%)
  local copies, waits for them, and re-layouts  13.8 us (7%)
  Pallas kernels  8.73 us (4%)
  other arithmetic  7.1 us (3%)
    ppermute x12, starting transfers between devices, from_partner(): return lax.ppermute(block, 'z', [(k, k ^ mask) for k in range(Z)])  51.2 us
    ppermute x12, waiting for transfers between devices, from_partner(): return lax.ppermute(block, 'z', [(k, k ^ mask) for k in range(Z)])  40.4 us
    all_to_all x6, starting transfers between devices, exchange(): return lax.all_to_all(block, axes, 0, 0, tiled=True)  38.9 us
    ppermute x3, starting transfers between devices, from_partner(): return lax.ppermute(block, 'h', [(0, 1), (1, 0)])  18.1 us
    ppermute x3, waiting for transfers between devices, from_partner(): return lax.ppermute(block, 'h', [(0, 1), (1, 0)])  13.5 us
    unnamed x52, local copies, waits for them, and re-layouts  10 us
    pallas_call x5, Pallas kernels, call(): pl.pallas_call(kernel, out_shape=outs, in_specs=ins, out_specs=[VMEM] * l...  8.73 us
    ppermute x3, starting transfers between devices, swap_core(): return lax.ppermute(block, 'c', [(0, 1), (1, 0)])  5.88 us
  transfers between devices with their start and end apart: 24, of which 16 were waited for; matrix products, arithmetic and copies ran while one was open for 3% of the time, Pallas kernels for 3%

profile of v2, /device:TPU:6, one launch (start us, length us, event | category | flops | bytes accessed | tf_op | source)
XLA Modules:
  0.0 207.5 jit_solution(15557634984790502864)
XLA Ops:
  2.6 9.5 %all-to-all-start = ((bf16[16,64,512]{2,1,0:T(8,128)(2,1)}), bf16[16,64,512]{2,1,0:T(8,128)(2,1)S(1)}, u32[]{:S(2)}, u32[]{:S(2)}) async-start(bf16[16,64,512]{2,1,0:T(8,128)(2,1)} %broadcast_in_dim.40), calls=%async_computation | async-start | bytes 2097152 | tf_op jit(solution)/shard_map/all_to_all | solution.py:34
  14.4 2.7 %collective-permute-start.5 = (f32[64,256]{1,0:T(8,128)S(1)}, f32[64,256]{1,0:T(8,128)S(1)}, u32[]{:S(2)}, u32[]{:S(2)}) collective-permute-start(f32[64,256]{1,0:T(8,128)S(1)} %fusion.6), channel_id=1, source_target_pairs={{0,1},{1,0},{2,3},{3,2},{4,5},{5,4},{6,7},{7,6},{8,9},{9,8},{10,11... | collective-permute-start | bytes 196616 | tf_op jit(solution)/shard_map/ppermute | solution.py:48
  17.1 3.6 %collective-permute-done.5 = f32[64,256]{1,0:T(8,128)S(1)} collective-permute-done((f32[64,256]{1,0:T(8,128)S(1)}, f32[64,256]{1,0:T(8,128)S(1)}, u32[]{:S(2)}, u32[]{:S(2)}) %collective-permute-start.5) | collective-permute-done | bytes 65568 | tf_op jit(solution)/shard_map/ppermute | solution.py:48
  20.8 5.2 %collective-permute-start.6 = (f32[64,256]{1,0:T(8,128)S(1)}, f32[64,256]{1,0:T(8,128)S(1)}, u32[]{:S(2)}, u32[]{:S(2)}) collective-permute-start(f32[64,256]{1,0:T(8,128)S(1)} %add.43), channel_id=1, source_target_pairs={{0,2},{1,3},{2,0},{3,1},{4,6},{5,7},{6,4},{7,5},{8,10},{9,11},{10,... | collective-permute-start | bytes 196616 | tf_op jit(solution)/shard_map/ppermute | solution.py:48
  26.0 3.6 %collective-permute-done.6 = f32[64,256]{1,0:T(8,128)S(1)} collective-permute-done((f32[64,256]{1,0:T(8,128)S(1)}, f32[64,256]{1,0:T(8,128)S(1)}, u32[]{:S(2)}, u32[]{:S(2)}) %collective-permute-start.6) | collective-permute-done | bytes 65568 | tf_op jit(solution)/shard_map/ppermute | solution.py:48
  29.6 8.7 %collective-permute-start.7 = (f32[64,256]{1,0:T(8,128)S(1)}, f32[64,256]{1,0:T(8,128)S(1)}, u32[]{:S(2)}, u32[]{:S(2)}) collective-permute-start(f32[64,256]{1,0:T(8,128)S(1)} %add.44), channel_id=1, source_target_pairs={{0,4},{1,5},{2,6},{3,7},{4,0},{5,1},{6,2},{7,3},{8,12},{9,13},{10,... | collective-permute-start | bytes 196616 | tf_op jit(solution)/shard_map/ppermute | solution.py:48
  42.8 5.0 %collective-permute-start.8 = (f32[64,256]{1,0:T(8,128)S(1)}, f32[64,256]{1,0:T(8,128)S(1)}, u32[]{:S(2)}, u32[]{:S(2)}) collective-permute-start(f32[64,256]{1,0:T(8,128)S(1)} %add.45), channel_id=1, source_target_pairs={{0,8},{8,0},{1,9},{9,1},{2,10},{10,2},{3,11},{11,3},{4,12},{12,4},... | collective-permute-start | bytes 196616 | tf_op jit(solution)/shard_map/ppermute | solution.py:47
  47.9 5.0 %collective-permute-done.8 = f32[64,256]{1,0:T(8,128)S(1)} collective-permute-done((f32[64,256]{1,0:T(8,128)S(1)}, f32[64,256]{1,0:T(8,128)S(1)}, u32[]{:S(2)}, u32[]{:S(2)}) %collective-permute-start.8) | collective-permute-done | bytes 65568 | tf_op jit(solution)/shard_map/ppermute | solution.py:47
  54.0 7.5 %all-to-all-start.1 = ((bf16[16,64,384]{2,1,0:T(8,128)(2,1)}), bf16[16,64,384]{2,1,0:T(8,128)(2,1)S(1)}, u32[]{:S(2)}, u32[]{:S(2)}) async-start(bf16[16,64,384]{2,1,0:T(8,128)(2,1)} %pad_maximum_fusion), calls=%async_computation.1 | async-start | bytes 1572864 | tf_op jit(solution)/shard_map/all_to_all | solution.py:34
  63.9 5.7 %collective-permute-start.2 = (bf16[1024,128]{1,0:T(8,128)(2,1)}, bf16[1024,128]{1,0:T(8,128)(2,1)S(1)}, u32[]{:S(2)}, u32[]{:S(2)}) collective-permute-start(bf16[1024,128]{1,0:T(8,128)(2,1)} %copy-done.18), channel_id=1, source_target_pairs={{0,2},{1,3},{2,0},{3,1},{4,6},{5,7},{6,4},{7,5},{8,10},{9,11},{10,... | collective-permute-start | bytes 786440 | tf_op jit(solution)/shard_map/ppermute | solution.py:48
  69.7 7.1 %collective-permute-start.3 = (bf16[1024,128]{1,0:T(8,128)(2,1)}, bf16[1024,128]{1,0:T(8,128)(2,1)}, u32[]{:S(2)}, u32[]{:S(2)}) collective-permute-start(bf16[1024,128]{1,0:T(8,128)(2,1)} %copy-done.17), channel_id=1, source_target_pairs={{0,4},{1,5},{2,6},{3,7},{4,0},{5,1},{6,2},{7,3},{8,12},{9,13},{10,... | collective-permute-start | bytes 786440 | tf_op jit(solution)/shard_map/ppermute | solution.py:48
  76.8 5.7 %collective-permute-start.4 = (bf16[1024,128]{1,0:T(8,128)(2,1)}, bf16[1024,128]{1,0:T(8,128)(2,1)}, u32[]{:S(2)}, u32[]{:S(2)}) collective-permute-start(bf16[1024,128]{1,0:T(8,128)(2,1)} %copy-done.16), channel_id=1, source_target_pairs={{0,8},{8,0},{1,9},{9,1},{2,10},{10,2},{3,11},{11,3},{4,12},{12,4},... | collective-permute-start | bytes 786440 | tf_op jit(solution)/shard_map/ppermute | solution.py:47
  82.6 6.6 %collective-permute-done.2.b = bf16[1024,128]{1,0:T(8,128)(2,1)S(1)} collective-permute-done((bf16[1024,128]{1,0:T(8,128)(2,1)}, bf16[1024,128]{1,0:T(8,128)(2,1)S(1)}, u32[]{:S(2)}, u32[]{:S(2)}) %collective-permute-start.2) | collective-permute-done | bytes 262176 | tf_op jit(solution)/shard_map/ppermute | solution.py:48
  91.3 3.5 %collective-permute-done.4.d = bf16[1024,128]{1,0:T(8,128)(2,1)} collective-permute-done((bf16[1024,128]{1,0:T(8,128)(2,1)}, bf16[1024,128]{1,0:T(8,128)(2,1)}, u32[]{:S(2)}, u32[]{:S(2)}) %collective-permute-start.4) | collective-permute-done | bytes 262176 | tf_op jit(solution)/shard_map/ppermute | solution.py:47
  99.5 7.6 %all-to-all-start.3 = ((bf16[32,32,256]{2,1,0:T(8,128)(2,1)}), bf16[32,32,256]{2,1,0:T(8,128)(2,1)}, u32[]{:S(2)}, u32[]{:S(2)}) async-start(bf16[32,32,256]{2,1,0:T(8,128)(2,1)} %bitcast.43), calls=%async_computation.3 | async-start | bytes 1048576 | tf_op jit(solution)/shard_map/all_to_all | solution.py:34
  107.1 7.3 %collective-permute-start.12 = (bf16[1024,128]{1,0:T(8,128)(2,1)S(1)}, bf16[1024,128]{1,0:T(8,128)(2,1)S(1)}, u32[]{:S(2)}, u32[]{:S(2)}) collective-permute-start(bf16[1024,128]{1,0:T(8,128)(2,1)S(1)} %get-tuple-element.25.a), channel_id=1, source_target_pairs={{0,8},{8,0},{1,9},{9,1},{2,10},{10,2},{3,11},{11,3},{4,12},{12,4},... | collective-permute-start | bytes 786440 | tf_op jit(solution)/shard_map/ppermute | solution.py:47
  114.4 3.4 %collective-permute-start.11 = (bf16[1024,128]{1,0:T(8,128)(2,1)S(1)}, bf16[1024,128]{1,0:T(8,128)(2,1)S(1)}, u32[]{:S(2)}, u32[]{:S(2)}) collective-permute-start(bf16[1024,128]{1,0:T(8,128)(2,1)S(1)} %get-tuple-element.25.a), channel_id=1, source_target_pairs={{0,4},{1,5},{2,6},{3,7},{4,0},{5,1},{6,2},{7,3},{8,12},{9,13},{10,... | collective-permute-start | bytes 786440 | tf_op jit(solution)/shard_map/ppermute | solution.py:48
  117.8 3.1 %collective-permute-start.10 = (bf16[1024,128]{1,0:T(8,128)(2,1)S(1)}, bf16[1024,128]{1,0:T(8,128)(2,1)S(1)}, u32[]{:S(2)}, u32[]{:S(2)}) collective-permute-start(bf16[1024,128]{1,0:T(8,128)(2,1)S(1)} %get-tuple-element.25.a), channel_id=1, source_target_pairs={{0,2},{1,3},{2,0},{3,1},{4,6},{5,7},{6,4},{7,5},{8,10},{9,11},{10,... | collective-permute-start | bytes 786440 | tf_op jit(solution)/shard_map/ppermute | solution.py:48
  120.9 4.4 %collective-permute-start.9 = (bf16[1024,128]{1,0:T(8,128)(2,1)S(1)}, bf16[1024,128]{1,0:T(8,128)(2,1)S(1)}, u32[]{:S(2)}, u32[]{:S(2)}) collective-permute-start(bf16[1024,128]{1,0:T(8,128)(2,1)S(1)} %get-tuple-element.25.a), channel_id=1, source_target_pairs={{0,1},{1,0},{2,3},{3,2},{4,5},{5,4},{6,7},{7,6},{8,9},{9,8},{10,11... | collective-permute-start | bytes 786440 | tf_op jit(solution)/shard_map/ppermute | solution.py:48
  125.3 5.0 %collective-permute-done.12.e = bf16[1024,128]{1,0:T(8,128)(2,1)S(1)} collective-permute-done((bf16[1024,128]{1,0:T(8,128)(2,1)S(1)}, bf16[1024,128]{1,0:T(8,128)(2,1)S(1)}, u32[]{:S(2)}, u32[]{:S(2)}) %collective-permute-start.12) | collective-permute-done | bytes 262176 | tf_op jit(solution)/shard_map/ppermute | solution.py:47
  130.3 2.9 %collective-permute-done.11.d = bf16[1024,128]{1,0:T(8,128)(2,1)S(1)} collective-permute-done((bf16[1024,128]{1,0:T(8,128)(2,1)S(1)}, bf16[1024,128]{1,0:T(8,128)(2,1)S(1)}, u32[]{:S(2)}, u32[]{:S(2)}) %collective-permute-start.11) | collective-permute-done | bytes 262176 | tf_op jit(solution)/shard_map/ppermute | solution.py:48
  133.2 6.3 %collective-permute-done.10.c = bf16[1024,128]{1,0:T(8,128)(2,1)S(1)} collective-permute-done((bf16[1024,128]{1,0:T(8,128)(2,1)S(1)}, bf16[1024,128]{1,0:T(8,128)(2,1)S(1)}, u32[]{:S(2)}, u32[]{:S(2)}) %collective-permute-start.10) | collective-permute-done | bytes 262176 | tf_op jit(solution)/shard_map/ppermute | solution.py:48
  139.4 2.5 %shard_map.104 = bf16[1024,512]{1,0:T(8,128)(2,1)} custom-call(s32[5]{0:T(128)S(1)} %select_reduce_fusion.slot_ref, bf16[1024,128]{1,0:T(8,128)(2,1)S(1)} %get-tuple-element.25.a, bf16[1024,128]{1,0:T(8,128)(2,1)S(1)} %collective-permute-done.9.b, bf16[1024,128]{1,0:T(8,128)(2,1)S(1)} %collective-permute-done.10.c, ...), custom_call_target="tpu_custom_call" | custom-call | flops 671088640 | bytes 3047444 | tf_op jit(solution)/shard_map/pallas_call | solution.py:62
  144.1 4.8 %all-to-all-start.2 = ((bf16[4,256,512]{2,1,0:T(8,128)(2,1)}), bf16[4,256,512]{2,1,0:T(8,128)(2,1)}, u32[]{:S(2)}, u32[]{:S(2)}) async-start(bf16[4,256,512]{2,1,0:T(8,128)(2,1)} %bitcast.12), calls=%async_computation.2 | async-start | bytes 2097152 | tf_op jit(solution)/shard_map/all_to_all | solution.py:34
  151.9 3.9 %collective-permute-done.13 = f32[32,256]{1,0:T(8,128)S(1)} collective-permute-done((f32[32,256]{1,0:T(8,128)S(1)}, f32[32,256]{1,0:T(8,128)S(1)}, u32[]{:S(2)}, u32[]{:S(2)}) %collective-permute-start.13) | collective-permute-done | bytes 32800 | tf_op jit(solution)/shard_map/ppermute | solution.py:48
  155.8 2.5 %collective-permute-start.14 = (f32[32,256]{1,0:T(8,128)S(1)}, f32[32,256]{1,0:T(8,128)S(1)}, u32[]{:S(2)}, u32[]{:S(2)}) collective-permute-start(f32[32,256]{1,0:T(8,128)S(1)} %add.47), channel_id=1, source_target_pairs={{0,2},{1,3},{2,0},{3,1},{4,6},{5,7},{6,4},{7,5},{8,10},{9,11},{10,... | collective-permute-start | bytes 98312 | tf_op jit(solution)/shard_map/ppermute | solution.py:48
  158.3 4.2 %collective-permute-done.14 = f32[32,256]{1,0:T(8,128)S(1)} collective-permute-done((f32[32,256]{1,0:T(8,128)S(1)}, f32[32,256]{1,0:T(8,128)S(1)}, u32[]{:S(2)}, u32[]{:S(2)}) %collective-permute-start.14) | collective-permute-done | bytes 32800 | tf_op jit(solution)/shard_map/ppermute | solution.py:48
  162.5 4.0 %collective-permute-start.15 = (f32[32,256]{1,0:T(8,128)S(1)}, f32[32,256]{1,0:T(8,128)S(1)}, u32[]{:S(2)}, u32[]{:S(2)}) collective-permute-start(f32[32,256]{1,0:T(8,128)S(1)} %add.48), channel_id=1, source_target_pairs={{0,4},{1,5},{2,6},{3,7},{4,0},{5,1},{6,2},{7,3},{8,12},{9,13},{10,... | collective-permute-start | bytes 98312 | tf_op jit(solution)/shard_map/ppermute | solution.py:48
  166.5 5.8 %collective-permute-done.15 = f32[32,256]{1,0:T(8,128)S(1)} collective-permute-done((f32[32,256]{1,0:T(8,128)S(1)}, f32[32,256]{1,0:T(8,128)S(1)}, u32[]{:S(2)}, u32[]{:S(2)}) %collective-permute-start.15) | collective-permute-done | bytes 32800 | tf_op jit(solution)/shard_map/ppermute | solution.py:48
  173.2 5.0 %all-to-all-start.4 = ((bf16[32,32,256]{2,1,0:T(8,128)(2,1)}), bf16[32,32,256]{2,1,0:T(8,128)(2,1)S(1)}, u32[]{:S(2)}, u32[]{:S(2)}) async-start(bf16[32,32,256]{2,1,0:T(8,128)(2,1)} %broadcast_in_dim.42), calls=%async_computation.4 | async-start | bytes 1048576 | tf_op jit(solution)/shard_map/all_to_all | solution.py:34
  192.1 4.5 %all-to-all-start.5 = ((bf16[4,64,512]{2,1,0:T(8,128)(2,1)}), bf16[4,64,512]{2,1,0:T(8,128)(2,1)S(1)}, u32[]{:S(2)}, u32[]{:S(2)}) async-start(bf16[4,64,512]{2,1,0:T(8,128)(2,1)} %bitcast.15), calls=%async_computation.5 | async-start | bytes 524288 | tf_op jit(solution)/shard_map/all_to_all | solution.py:34
  200.4 5.4 %all-to-all-done.5 = bf16[4,64,512]{2,1,0:T(8,128)(2,1)S(1)} async-done(((bf16[4,64,512]{2,1,0:T(8,128)(2,1)}), bf16[4,64,512]{2,1,0:T(8,128)(2,1)S(1)}, u32[]{:S(2)}, u32[]{:S(2)}) %all-to-all-start.5) | async-done | bytes 262176 | tf_op jit(solution)/shard_map/all_to_all | solution.py:34
  (99 shorter events, 44.3 us)
Async XLA Ops:
  0.6 47.2 %copy-start = (bf16[1,2048,64]{1,2,0:T(8,128)(2,1)S(1)}, bf16[1,2048,64]{1,2,0:T(8,128)(2,1)}, u32[]{:S(2)}) copy-start(bf16[1,2048,64]{1,2,0:T(8,128)(2,1)} %param.12) | copy-start | bytes 786436
  2.6 11.5 %copy-start.20 = (bf16[512,256]{1,0:T(8,128)(2,1)S(1)}, bf16[512,256]{1,0:T(8,128)(2,1)}, u32[]{:S(2)}) copy-start(bf16[512,256]{1,0:T(8,128)(2,1)} %param.10) | copy-start | bytes 786436
  2.6 11.5 %copy-start.23 = (bf16[64,512]{1,0:T(8,128)(2,1)S(1)}, bf16[64,512]{1,0:T(8,128)(2,1)}, u32[]{:S(2)}) copy-start(bf16[64,512]{1,0:T(8,128)(2,1)} %param.7) | copy-start | bytes 196612
  2.6 37.9 %all-to-all-start = ((bf16[16,64,512]{2,1,0:T(8,128)(2,1)}), bf16[16,64,512]{2,1,0:T(8,128)(2,1)S(1)}, u32[]{:S(2)}, u32[]{:S(2)}) async-start(bf16[16,64,512]{2,1,0:T(8,128)(2,1)} %broadcast_in_dim.40), calls=%async_computation | async-start | bytes 2097152 | tf_op jit(solution)/shard_map/all_to_all | solution.py:34
  12.2 13.8 %copy-start.25 = (s32[5]{0:T(128)S(1)}, s32[5]{0:T(128)}, u32[]{:S(2)}) copy-start(s32[5]{0:T(128)} %constant.37.clone) | copy-start | bytes 64
  12.2 26.1 %copy-start.24 = (s32[1,5]{1,0:T(1,128)S(1)}, s32[1,5]{1,0:T(1,128)}, u32[]{:S(2)}) copy-start(s32[1,5]{1,0:T(1,128)} %param.9) | copy-start | bytes 64
  12.2 17.4 %collective-permute-start = (bf16[352,512]{1,0:T(8,128)(2,1)S(1)}, bf16[352,512]{1,0:T(8,128)(2,1)S(1)}, u32[]{:S(2)}, u32[]{:S(2)}) collective-permute-start(bf16[352,512]{1,0:T(8,128)(2,1)S(1)} %maximum_maximum_fusion), channel_id=1, source_target_pairs={{0,16},{16,0},{1,17},{17,1},{2,18},{18,2},{3,19},{19,3},{4,20},{20... | collective-permute-start | bytes 1081352 | tf_op jit(solution)/shard_map/ppermute | solution.py:42
  14.4 6.4 %collective-permute-start.5 = (f32[64,256]{1,0:T(8,128)S(1)}, f32[64,256]{1,0:T(8,128)S(1)}, u32[]{:S(2)}, u32[]{:S(2)}) collective-permute-start(f32[64,256]{1,0:T(8,128)S(1)} %fusion.6), channel_id=1, source_target_pairs={{0,1},{1,0},{2,3},{3,2},{4,5},{5,4},{6,7},{7,6},{8,9},{9,8},{10,11... | collective-permute-start | bytes 196616 | tf_op jit(solution)/shard_map/ppermute | solution.py:48
  20.8 8.8 %collective-permute-start.6 = (f32[64,256]{1,0:T(8,128)S(1)}, f32[64,256]{1,0:T(8,128)S(1)}, u32[]{:S(2)}, u32[]{:S(2)}) collective-permute-start(f32[64,256]{1,0:T(8,128)S(1)} %add.43), channel_id=1, source_target_pairs={{0,2},{1,3},{2,0},{3,1},{4,6},{5,7},{6,4},{7,5},{8,10},{9,11},{10,... | collective-permute-start | bytes 196616 | tf_op jit(solution)/shard_map/ppermute | solution.py:48
  29.6 10.9 %collective-permute-start.7 = (f32[64,256]{1,0:T(8,128)S(1)}, f32[64,256]{1,0:T(8,128)S(1)}, u32[]{:S(2)}, u32[]{:S(2)}) collective-permute-start(f32[64,256]{1,0:T(8,128)S(1)} %add.44), channel_id=1, source_target_pairs={{0,4},{1,5},{2,6},{3,7},{4,0},{5,1},{6,2},{7,3},{8,12},{9,13},{10,... | collective-permute-start | bytes 196616 | tf_op jit(solution)/shard_map/ppermute | solution.py:48
  42.8 11.2 %copy-start.16 = (bf16[1024,128]{1,0:T(8,128)(2,1)}, bf16[1024,128]{1,0:T(8,128)(2,1)S(1)}, u32[]{:S(2)}) copy-start(bf16[1024,128]{1,0:T(8,128)(2,1)S(1)} %get-tuple-element.22) | copy-start | bytes 786436
  42.8 18.7 %copy-start.18 = (bf16[1024,128]{1,0:T(8,128)(2,1)}, bf16[1024,128]{1,0:T(8,128)(2,1)S(1)}, u32[]{:S(2)}) copy-start(bf16[1024,128]{1,0:T(8,128)(2,1)S(1)} %get-tuple-element.20) | copy-start | bytes 786436
  42.8 21.1 %copy-start.17 = (bf16[1024,128]{1,0:T(8,128)(2,1)}, bf16[1024,128]{1,0:T(8,128)(2,1)S(1)}, u32[]{:S(2)}) copy-start(bf16[1024,128]{1,0:T(8,128)(2,1)S(1)} %get-tuple-element.21) | copy-start | bytes 786436
  42.8 10.1 %collective-permute-start.8 = (f32[64,256]{1,0:T(8,128)S(1)}, f32[64,256]{1,0:T(8,128)S(1)}, u32[]{:S(2)}, u32[]{:S(2)}) collective-permute-start(f32[64,256]{1,0:T(8,128)S(1)} %add.45), channel_id=1, source_target_pairs={{0,8},{8,0},{1,9},{9,1},{2,10},{10,2},{3,11},{11,3},{4,12},{12,4},... | collective-permute-start | bytes 196616 | tf_op jit(solution)/shard_map/ppermute | solution.py:47
  54.0 40.8 %all-to-all-start.1 = ((bf16[16,64,384]{2,1,0:T(8,128)(2,1)}), bf16[16,64,384]{2,1,0:T(8,128)(2,1)S(1)}, u32[]{:S(2)}, u32[]{:S(2)}) async-start(bf16[16,64,384]{2,1,0:T(8,128)(2,1)} %pad_maximum_fusion), calls=%async_computation.1 | async-start | bytes 1572864 | tf_op jit(solution)/shard_map/all_to_all | solution.py:34
  61.5 21.1 %collective-permute-start.1 = (bf16[1024,128]{1,0:T(8,128)(2,1)}, bf16[1024,128]{1,0:T(8,128)(2,1)S(1)}, u32[]{:S(2)}, u32[]{:S(2)}) collective-permute-start(bf16[1024,128]{1,0:T(8,128)(2,1)} %copy-done.19), channel_id=1, source_target_pairs={{0,1},{1,0},{2,3},{3,2},{4,5},{5,4},{6,7},{7,6},{8,9},{9,8},{10,11... | collective-permute-start | bytes 786440 | tf_op jit(solution)/shard_map/ppermute | solution.py:48
  63.9 25.2 %collective-permute-start.2 = (bf16[1024,128]{1,0:T(8,128)(2,1)}, bf16[1024,128]{1,0:T(8,128)(2,1)S(1)}, u32[]{:S(2)}, u32[]{:S(2)}) collective-permute-start(bf16[1024,128]{1,0:T(8,128)(2,1)} %copy-done.18), channel_id=1, source_target_pairs={{0,2},{1,3},{2,0},{3,1},{4,6},{5,7},{6,4},{7,5},{8,10},{9,11},{10,... | collective-permute-start | bytes 786440 | tf_op jit(solution)/shard_map/ppermute | solution.py:48
  69.7 21.7 %collective-permute-start.3 = (bf16[1024,128]{1,0:T(8,128)(2,1)}, bf16[1024,128]{1,0:T(8,128)(2,1)}, u32[]{:S(2)}, u32[]{:S(2)}) collective-permute-start(bf16[1024,128]{1,0:T(8,128)(2,1)} %copy-done.17), channel_id=1, source_target_pairs={{0,4},{1,5},{2,6},{3,7},{4,0},{5,1},{6,2},{7,3},{8,12},{9,13},{10,... | collective-permute-start | bytes 786440 | tf_op jit(solution)/shard_map/ppermute | solution.py:48
  76.8 18.1 %collective-permute-start.4 = (bf16[1024,128]{1,0:T(8,128)(2,1)}, bf16[1024,128]{1,0:T(8,128)(2,1)}, u32[]{:S(2)}, u32[]{:S(2)}) collective-permute-start(bf16[1024,128]{1,0:T(8,128)(2,1)} %copy-done.16), channel_id=1, source_target_pairs={{0,8},{8,0},{1,9},{9,1},{2,10},{10,2},{3,11},{11,3},{4,12},{12,4},... | collective-permute-start | bytes 786440 | tf_op jit(solution)/shard_map/ppermute | solution.py:47
  99.5 44.6 %all-to-all-start.3 = ((bf16[32,32,256]{2,1,0:T(8,128)(2,1)}), bf16[32,32,256]{2,1,0:T(8,128)(2,1)}, u32[]{:S(2)}, u32[]{:S(2)}) async-start(bf16[32,32,256]{2,1,0:T(8,128)(2,1)} %bitcast.43), calls=%async_computation.3 | async-start | bytes 1048576 | tf_op jit(solution)/shard_map/all_to_all | solution.py:34
  107.1 23.2 %collective-permute-start.12 = (bf16[1024,128]{1,0:T(8,128)(2,1)S(1)}, bf16[1024,128]{1,0:T(8,128)(2,1)S(1)}, u32[]{:S(2)}, u32[]{:S(2)}) collective-permute-start(bf16[1024,128]{1,0:T(8,128)(2,1)S(1)} %get-tuple-element.25.a), channel_id=1, source_target_pairs={{0,8},{8,0},{1,9},{9,1},{2,10},{10,2},{3,11},{11,3},{4,12},{12,4},... | collective-permute-start | bytes 786440 | tf_op jit(solution)/shard_map/ppermute | solution.py:47
  114.4 18.8 %collective-permute-start.11 = (bf16[1024,128]{1,0:T(8,128)(2,1)S(1)}, bf16[1024,128]{1,0:T(8,128)(2,1)S(1)}, u32[]{:S(2)}, u32[]{:S(2)}) collective-permute-start(bf16[1024,128]{1,0:T(8,128)(2,1)S(1)} %get-tuple-element.25.a), channel_id=1, source_target_pairs={{0,4},{1,5},{2,6},{3,7},{4,0},{5,1},{6,2},{7,3},{8,12},{9,13},{10,... | collective-permute-start | bytes 786440 | tf_op jit(solution)/shard_map/ppermute | solution.py:48
  117.8 21.7 %collective-permute-start.10 = (bf16[1024,128]{1,0:T(8,128)(2,1)S(1)}, bf16[1024,128]{1,0:T(8,128)(2,1)S(1)}, u32[]{:S(2)}, u32[]{:S(2)}) collective-permute-start(bf16[1024,128]{1,0:T(8,128)(2,1)S(1)} %get-tuple-element.25.a), channel_id=1, source_target_pairs={{0,2},{1,3},{2,0},{3,1},{4,6},{5,7},{6,4},{7,5},{8,10},{9,11},{10,... | collective-permute-start | bytes 786440 | tf_op jit(solution)/shard_map/ppermute | solution.py:48
  120.9 18.6 %collective-permute-start.9 = (bf16[1024,128]{1,0:T(8,128)(2,1)S(1)}, bf16[1024,128]{1,0:T(8,128)(2,1)S(1)}, u32[]{:S(2)}, u32[]{:S(2)}) collective-permute-start(bf16[1024,128]{1,0:T(8,128)(2,1)S(1)} %get-tuple-element.25.a), channel_id=1, source_target_pairs={{0,1},{1,0},{2,3},{3,2},{4,5},{5,4},{6,7},{7,6},{8,9},{9,8},{10,11... | collective-permute-start | bytes 786440 | tf_op jit(solution)/shard_map/ppermute | solution.py:48
  144.1 28.3 %all-to-all-start.2 = ((bf16[4,256,512]{2,1,0:T(8,128)(2,1)}), bf16[4,256,512]{2,1,0:T(8,128)(2,1)}, u32[]{:S(2)}, u32[]{:S(2)}) async-start(bf16[4,256,512]{2,1,0:T(8,128)(2,1)} %bitcast.12), calls=%async_computation.2 | async-start | bytes 2097152 | tf_op jit(solution)/shard_map/all_to_all | solution.py:34
  150.0 5.8 %collective-permute-start.13 = (f32[32,256]{1,0:T(8,128)S(1)}, f32[32,256]{1,0:T(8,128)S(1)}, u32[]{:S(2)}, u32[]{:S(2)}) collective-permute-start(f32[32,256]{1,0:T(8,128)S(1)} %convert_reduce_fusion), channel_id=1, source_target_pairs={{0,1},{1,0},{2,3},{3,2},{4,5},{5,4},{6,7},{7,6},{8,9},{9,8},{10,11... | collective-permute-start | bytes 98312 | tf_op jit(solution)/shard_map/ppermute | solution.py:48
  155.8 6.7 %collective-permute-start.14 = (f32[32,256]{1,0:T(8,128)S(1)}, f32[32,256]{1,0:T(8,128)S(1)}, u32[]{:S(2)}, u32[]{:S(2)}) collective-permute-start(f32[32,256]{1,0:T(8,128)S(1)} %add.47), channel_id=1, source_target_pairs={{0,2},{1,3},{2,0},{3,1},{4,6},{5,7},{6,4},{7,5},{8,10},{9,11},{10,... | collective-permute-start | bytes 98312 | tf_op jit(solution)/shard_map/ppermute | solution.py:48
  162.5 9.9 %collective-permute-start.15 = (f32[32,256]{1,0:T(8,128)S(1)}, f32[32,256]{1,0:T(8,128)S(1)}, u32[]{:S(2)}, u32[]{:S(2)}) collective-permute-start(f32[32,256]{1,0:T(8,128)S(1)} %add.48), channel_id=1, source_target_pairs={{0,4},{1,5},{2,6},{3,7},{4,0},{5,1},{6,2},{7,3},{8,12},{9,13},{10,... | collective-permute-start | bytes 98312 | tf_op jit(solution)/shard_map/ppermute | solution.py:48
  173.2 18.8 %all-to-all-start.4 = ((bf16[32,32,256]{2,1,0:T(8,128)(2,1)}), bf16[32,32,256]{2,1,0:T(8,128)(2,1)S(1)}, u32[]{:S(2)}, u32[]{:S(2)}) async-start(bf16[32,32,256]{2,1,0:T(8,128)(2,1)} %broadcast_in_dim.42), calls=%async_computation.4 | async-start | bytes 1048576 | tf_op jit(solution)/shard_map/all_to_all | solution.py:34
  184.4 4.4 %collective-permute-start.16 = (f32[352,512]{1,0:T(8,128)}, f32[352,512]{1,0:T(8,128)S(1)}, u32[]{:S(2)}, u32[]{:S(2)}) collective-permute-start(f32[352,512]{1,0:T(8,128)} %get-tuple-element.30), channel_id=1, source_target_pairs={{0,16},{16,0},{1,17},{17,1},{2,18},{18,2},{3,19},{19,3},{4,20},{20... | collective-permute-start | bytes 2162696 | tf_op jit(solution)/shard_map/ppermute | solution.py:42
  192.1 13.7 %all-to-all-start.5 = ((bf16[4,64,512]{2,1,0:T(8,128)(2,1)}), bf16[4,64,512]{2,1,0:T(8,128)(2,1)S(1)}, u32[]{:S(2)}, u32[]{:S(2)}) async-start(bf16[4,64,512]{2,1,0:T(8,128)(2,1)} %bitcast.15), calls=%async_computation.5 | async-start | bytes 524288 | tf_op jit(solution)/shard_map/all_to_all | solution.py:34
  197.8 8.8 %collective-permute-start.17 = (f32[512,256]{1,0:T(8,128)S(1)}, f32[512,256]{1,0:T(8,128)S(1)}, u32[]{:S(2)}, u32[]{:S(2)}) collective-permute-start(f32[512,256]{1,0:T(8,128)S(1)} %shard_map.106), channel_id=1, source_target_pairs={{0,16},{16,0},{1,17},{17,1},{2,18},{18,2},{3,19},{19,3},{4,20},{20... | collective-permute-start | bytes 1572872 | tf_op jit(solution)/shard_map/ppermute | solution.py:42
  (18 other events, 54.3 us)

commit v3 on v2

--- a/solution.py
+++ b/solution.py
@@ -48,6 +48,10 @@
     return lax.ppermute(block, "z", [(k, k ^ mask) for k in range(Z)])
 
 
+def to_x(block, shift):
+    return lax.ppermute(block, "x", [(k, (k + shift) % X) for k in range(X)])
+
+
 def after(value, *others):
     return lax.optimization_barrier((value, *others))[0]
 
@@ -87,14 +91,26 @@
     return jnp.concatenate([factor_ref[...], last[:, :RANK], last[:, RANK:]], axis=0)
 
 
-def forward_kernel(slot_ref, tile_ref, mine_ref, other_ref, *outs):
+def place_of(x, shift):
+    return pl.ds(pl.multiple_of(lax.rem(x + shift, X) * STEP, STEP), STEP)
+
+
+def forward_kernel(slot_ref, x_ref, t0, t1, t2, t3, mine_ref, other_ref, tile_ref, *outs):
     weights = all_weights(slot_ref, mine_ref, other_ref)
-    for part in range(X):
-        rows = pl.ds(part * STEP, STEP)
-        products = dot(tile_ref[rows, :], weights, 1, 1)
+    for shift, part in enumerate((t0, t1, t2, t3)):
+        rows = place_of(x_ref[0], X - shift)
+        tile_ref[rows, :] = part[...]
+        products = dot(part[...], weights, 1, 1)
         outs[0][rows, :] = products[:, :COLS]
         for kind in range(1, SLOTS):
             outs[kind][rows, :] = products[:, kind * COLS : (kind + 1) * COLS].astype(BF16)
+
+
+def low_kernel(hidden_ref, sent_ref, factor_ref, other_ref, out_ref):
+    factor = all_factor(factor_ref, other_ref)
+    for part in range(X):
+        rows = pl.ds(part * STEP, STEP)
+        out_ref[rows, :] = hidden_ref[rows, :] + dot(sent_ref[rows, COLS:], factor, 1, 1)
 
 
 def hidden_kernel(core_ref, hidden_ref, a, b, c, d, sent_ref, factor_ref, other_ref, dpre_ref, back_ref):
@@ -105,7 +121,6 @@
         hidden = hidden_ref[rows, :]
         for arrived in (a, b, c, d):
             hidden = hidden + arrived[rows, :].astype(F32)
-        hidden = hidden + dot(sent_ref[rows, COLS:], factor, 1, 1)
         up = sent_ref[rows, :COLS].astype(F32)
         up = jnp.where(core == 0, up, pltpu.roll(up, OWN, 1))
         dpre = (up * gelu_slope(hidden)).astype(BF16)
@@ -113,12 +128,16 @@
         back_ref[rows, :] = dot(dpre, factor, 1, 0).astype(BF16)
 
 
-def input_kernel(slot_ref, a, b, c, d, e, mine_ref, other_ref, out_ref):
+def input_kernel(slot_ref, x_ref, a, b, c, d, e, mine_ref, other_ref, own_ref, *outs):
     weights = all_weights(slot_ref, mine_ref, other_ref)
-    for part in range(X):
-        rows = pl.ds(part * STEP, STEP)
+    for shift in (2, 1, 3, 0):
+        rows = place_of(x_ref[0], shift)
         stacked = jnp.concatenate([k[rows, :] for k in (a, b, c, d, e)], axis=1)
-        out_ref[rows, :] = dot(stacked, weights, 1, 0).astype(BF16)
+        result = dot(stacked, weights, 1, 0)
+        if shift == 0:
+            own_ref[...] = result
+        else:
+            outs[shift - 1][...] = result.astype(BF16)
 
 
 def weight_kernel(slot_ref, a, b, c, d, e, tile_ref, sent_ref, keep_ref, away_ref, factor_ref):
@@ -139,60 +158,72 @@
 
 def body(inputs, block_weights, partners, code_in, code_out, upstream):
     core = lax.axis_index("c").reshape(1)
+    place = lax.axis_index("x").reshape(1)
     row = lax.axis_index("h") * Z + lax.axis_index("z")
+    own = (lax.axis_index("x") * Y + lax.axis_index("y")) * OWN
+    inputs, core, place, row, own = lax.optimization_barrier((inputs, core, place, row, own))
 
     targets = jnp.bitwise_xor(row, jnp.array(MASKS, jnp.int32))
     slots = jnp.sum(
         jnp.where(partners[0][None, :] == targets[:, None], jnp.arange(SLOTS)[None, :], 0), axis=1
     ).astype(jnp.int32)
 
-    tile = spread(inputs, ("x", "y"), PEERS).reshape(TOKENS, ROWS)
-
     factor = code_out[:, 0, :].T
     packed = jnp.concatenate([factor[: OWN // 2], factor[OWN // 2 :]], axis=1)
     mine = block_weights[0]
     other = swap_core(jnp.concatenate([mine.reshape(SLOTS * OWN, ROWS), packed], axis=0))
 
-    codes = dot(inputs, code_in, 1, 0)
-    for mask in (1, 2):
-        codes = codes + from_partner(codes, mask)
-    codes = after(codes, other)
-    codes = codes + from_partner(codes, 4)
+    near = spread(inputs, ("y",), Y).reshape(Y * OWN, ROWS)
+    near = after(near, other)
+    far = [to_x(near, shift) for shift in range(1, X)]
+
+    codes = dot(inputs, code_in, 1, 0).astype(BF16)
+    codes = spread(after(codes, near), ("h", "z"), H * Z)
+    codes = codes.astype(F32).sum(0).astype(BF16)
+    near = after(near, codes)
 
     tall = [shape((TOKENS, COLS), BF16)] * 4
-    hidden, *terms = call(
-        forward_kernel, [SMEM] + [VMEM] * 3, [shape((TOKENS, COLS), F32)] + tall,
-        2 * TOKENS * COLS * SLOTS * ROWS, slots, tile, mine, other,
-    )
-    codes = after(codes, hidden)
-    codes = (codes + from_partner(codes, 8)).astype(BF16)
+    tile, hidden, *terms = call(
+        forward_kernel, [SMEM] * 2 + [VMEM] * 6,
+        [shape((TOKENS, ROWS), BF16), shape((TOKENS, COLS), F32)] + tall,
+        2 * TOKENS * COLS * SLOTS * ROWS, slots, place, near, *far, mine, other,
+    )
     arrived = [from_partner(term, mask) for term, mask in zip(terms, MASKS[1:])]
 
     sent = upstream[0].T.reshape(OWN, PEERS, COLS).transpose(1, 0, 2)
     sent = jnp.concatenate([sent, jnp.broadcast_to(codes[None], (PEERS, OWN, RANK))], axis=2)
-    sent = exchange(sent, ("x", "y")).reshape(TOKENS, COLS + RANK)
+    sent = exchange(after(sent, hidden), ("x", "y")).reshape(TOKENS, COLS + RANK)
+    (hidden,) = call(
+        low_kernel, [VMEM] * 4, [shape((TOKENS, COLS), F32)],
+        2 * TOKENS * COLS * RANK, hidden, sent, factor, other,
+    )
+    arrived = lax.optimization_barrier((hidden, *arrived))[1:]
     dpre, back = call(
         hidden_kernel, [SMEM] + [VMEM] * 8,
         [shape((TOKENS, COLS), BF16), shape((TOKENS, RANK), BF16)],
-        4 * TOKENS * COLS * RANK, core, hidden, *arrived, sent, factor, other,
+        2 * TOKENS * COLS * RANK, core, hidden, *arrived, sent, factor, other,
     )
     kinds = [dpre] + [from_partner(dpre, mask) for mask in MASKS[1:]]
 
     back = exchange(back.reshape(PEERS * H, OWN // H, RANK), ("x", "y", "h")).astype(F32).sum(0)
 
-    (partial,) = call(
-        input_kernel, [SMEM] + [VMEM] * 7, [shape((TOKENS, ROWS), BF16)],
-        2 * TOKENS * COLS * SLOTS * ROWS, slots, *kinds, mine, other,
-    )
-    back = after(back, partial)
-    partial = exchange(partial.reshape(X, Y * OWN, ROWS), ("x",)).astype(F32).sum(0).astype(BF16)
-    for mask in MASKS[1:4]:
-        back = back + from_partner(back, mask)
-    back = spread(back.astype(BF16), ("x", "y", "h"), PEERS * H).reshape(TOKENS, RANK)
+    back = back.astype(BF16)
+    back = spread(back, ("z",), Z).astype(F32).sum(0).astype(BF16)
+    kinds = lax.optimization_barrier((back, *kinds))[1:]
+    back = spread(back, ("x", "y", "h"), PEERS * H).reshape(TOKENS, RANK)
+
+    partial, *away = call(
+        input_kernel, [SMEM] * 2 + [VMEM] * 7,
+        [shape((STEP, ROWS), F32)] + [shape((STEP, ROWS), BF16)] * 3,
+        2 * TOKENS * COLS * SLOTS * ROWS, slots, place, *kinds, mine, other,
+    )
+    came = [to_x(part, shift) for shift, part in enumerate(away, 1)]
+    kinds = lax.optimization_barrier((*kinds, *came))[:SLOTS]
+    for part in came:
+        partial = partial + part.astype(F32)
     partial = after(partial, back)
-    partial = exchange(partial.reshape(Y, OWN, ROWS), ("y",))
-    place = (lax.axis_index("x") * Y + lax.axis_index("y")) * OWN
-    own_back = lax.dynamic_slice_in_dim(back, place, OWN, 0)
+    partial = exchange(partial.astype(BF16).reshape(Y, OWN, ROWS), ("y",))
+    own_back = lax.dynamic_slice_in_dim(back, own, OWN, 0)
     input_grad = partial.astype(F32).sum(0) + dot(own_back, code_in, 1, 1)
     input_grad = input_grad.astype(BF16)
 

time: 209 us -> 192 us (0.919)
  waiting for transfers between devices: 61.8 us -> 29.5 us
  blocking collectives: 0 us -> 13.2 us
    ppermute x12 -> x6, waiting for transfers between devices: 40.4 us -> 9.56 us  [from_partner(): return lax.ppermute(block, 'z', [(k, k ^ mask) for k in range(Z)])]
    ppermute x12 -> x6, starting transfers between devices: 51.2 us -> 24.6 us  [from_partner(): return lax.ppermute(block, 'z', [(k, k ^ mask) for k in range(Z)])]
    ppermute x0 -> x6, starting transfers between devices: none -> 18.5 us  [to_x(): return lax.ppermute(block, 'x', [(k, (k + shift) % X) for k in range(X)])]
    ppermute x3 -> x2, waiting for transfers between devices: 13.5 us -> 0.01 us  [from_partner(): return lax.ppermute(block, 'h', [(0, 1), (1, 0)])]
    all_to_all x0 -> x1, blocking collectives: none -> 13.2 us  [exchange(): return lax.all_to_all(block, axes, 0, 0, tiled=True)]
    all_to_all x6, waiting for transfers between devices: 5.47 us -> 18.1 us  [exchange(): return lax.all_to_all(block, axes, 0, 0, tiled=True)]
    all_to_all x6, starting transfers between devices: 38.9 us -> 50.1 us  [exchange(): return lax.all_to_all(block, axes, 0, 0, tiled=True)]
    ppermute x3 -> x2, starting transfers between devices: 18.1 us -> 13.2 us  [from_partner(): return lax.ppermute(block, 'h', [(0, 1), (1, 0)])]
  transfers between devices with their start and end apart: 24 -> 23, of which waited for: 16 -> 7; matrix products, arithmetic and copies ran while one was open for 3% -> 6% of each run, Pallas kernels for 3% -> 2%
where the time goes in v3:
time: 192 us; the launch traced here: 191 us
  starting transfers between devices  112 us (58%)
  waiting for transfers between devices  29.5 us (15%)
  local copies, waits for them, and re-layouts  15.4 us (8%)
  blocking collectives  13.2 us (7%)
  Pallas kernels  10.6 us (6%)
  other arithmetic  7.71 us (4%)
    all_to_all x6, starting transfers between devices, exchange(): return lax.all_to_all(block, axes, 0, 0, tiled=True)  50.1 us
    ppermute x6, starting transfers between devices, from_partner(): return lax.ppermute(block, 'z', [(k, k ^ mask) for k in range(Z)])  24.6 us
    ppermute x6, starting transfers between devices, to_x(): return lax.ppermute(block, 'x', [(k, (k + shift) % X) for k in range(X)])  18.5 us
    all_to_all x6, waiting for transfers between devices, exchange(): return lax.all_to_all(block, axes, 0, 0, tiled=True)  18.1 us
    all_to_all x1, blocking collectives, exchange(): return lax.all_to_all(block, axes, 0, 0, tiled=True)  13.2 us
    ppermute x2, starting transfers between devices, from_partner(): return lax.ppermute(block, 'h', [(0, 1), (1, 0)])  13.2 us
    pallas_call x6, Pallas kernels, call(): pl.pallas_call(kernel, out_shape=outs, in_specs=ins, out_specs=[VMEM] * l...  10.6 us
    ppermute x6, waiting for transfers between devices, from_partner(): return lax.ppermute(block, 'z', [(k, k ^ mask) for k in range(Z)])  9.56 us
  transfers between devices with their start and end apart: 23, of which 7 were waited for; matrix products, arithmetic and copies ran while one was open for 6% of the time, Pallas kernels for 2%

profile of v3, /device:TPU:6, one launch (start us, length us, event | category | flops | bytes accessed | tf_op | source)
XLA Modules:
  0.0 190.7 jit_solution(1996557661502052308)
XLA Ops:
  2.3 4.9 %all-to-all-start = ((bf16[4,64,512]{2,1,0:T(8,128)(2,1)}), bf16[4,64,512]{2,1,0:T(8,128)(2,1)S(1)}, u32[]{:S(2)}, u32[]{:S(2)}) async-start(bf16[4,64,512]{2,1,0:T(8,128)(2,1)} %broadcast_in_dim.28), calls=%async_computation | async-start | bytes 524288 | tf_op jit(solution)/shard_map/all_to_all | solution.py:34
  8.0 1.9 %collective-permute-start = (bf16[352,512]{1,0:T(8,128)(2,1)S(1)}, bf16[352,512]{1,0:T(8,128)(2,1)S(1)}, u32[]{:S(2)}, u32[]{:S(2)}) collective-permute-start(bf16[352,512]{1,0:T(8,128)(2,1)S(1)} %maximum_maximum_fusion), channel_id=1, source_target_pairs={{0,16},{16,0},{1,17},{17,1},{2,18},{18,2},{3,19},{19,3},{4,20},{20... | collective-permute-start | bytes 1081352 | tf_op jit(solution)/shard_map/ppermute | solution.py:42
  11.5 4.6 %all-to-all-done = bf16[4,64,512]{2,1,0:T(8,128)(2,1)S(1)} async-done(((bf16[4,64,512]{2,1,0:T(8,128)(2,1)}), bf16[4,64,512]{2,1,0:T(8,128)(2,1)S(1)}, u32[]{:S(2)}, u32[]{:S(2)}) %all-to-all-start) | async-done | bytes 262176 | tf_op jit(solution)/shard_map/all_to_all | solution.py:34
  17.0 14.5 %all-to-all-start.1 = ((bf16[16,64,256]{2,1,0:T(8,128)(2,1)}), bf16[16,64,256]{2,1,0:T(8,128)(2,1)S(1)}, u32[]{:S(2)}, u32[]{:S(2)}) async-start(bf16[16,64,256]{2,1,0:T(8,128)(2,1)} %broadcast_in_dim.29), calls=%async_computation.1 | async-start | bytes 1048576 | tf_op jit(solution)/shard_map/all_to_all | solution.py:34
  31.5 2.4 %collective-permute-start.1 = (bf16[256,512]{1,0:T(8,128)(2,1)S(1)}, bf16[256,512]{1,0:T(8,128)(2,1)S(1)}, u32[]{:S(2)}, u32[]{:S(2)}) collective-permute-start(bf16[256,512]{1,0:T(8,128)(2,1)S(1)} %bitcast.44), channel_id=1, source_target_pairs={{0,128},{128,256},{256,384},{384,0},{1,129},{129,257},{257,385},{3... | collective-permute-start | bytes 786440 | tf_op jit(solution)/shard_map/ppermute | solution.py:52
  33.9 4.3 %collective-permute-start.2 = (bf16[256,512]{1,0:T(8,128)(2,1)S(1)}, bf16[256,512]{1,0:T(8,128)(2,1)S(1)}, u32[]{:S(2)}, u32[]{:S(2)}) collective-permute-start(bf16[256,512]{1,0:T(8,128)(2,1)S(1)} %bitcast.45), channel_id=1, source_target_pairs={{0,256},{128,384},{256,0},{384,128},{1,257},{129,385},{257,1},{385... | collective-permute-start | bytes 786440 | tf_op jit(solution)/shard_map/ppermute | solution.py:52
  38.3 1.9 %collective-permute-start.3 = (bf16[256,512]{1,0:T(8,128)(2,1)S(1)}, bf16[256,512]{1,0:T(8,128)(2,1)S(1)}, u32[]{:S(2)}, u32[]{:S(2)}) collective-permute-start(bf16[256,512]{1,0:T(8,128)(2,1)S(1)} %bitcast.46), channel_id=1, source_target_pairs={{0,384},{128,0},{256,128},{384,256},{1,385},{129,1},{257,129},{385... | collective-permute-start | bytes 786440 | tf_op jit(solution)/shard_map/ppermute | solution.py:52
  40.4 7.5 %all-to-all-done.1 = bf16[16,64,256]{2,1,0:T(8,128)(2,1)S(1)} async-done(((bf16[16,64,256]{2,1,0:T(8,128)(2,1)}), bf16[16,64,256]{2,1,0:T(8,128)(2,1)S(1)}, u32[]{:S(2)}, u32[]{:S(2)}) %all-to-all-start.1) | async-done | bytes 524320 | tf_op jit(solution)/shard_map/all_to_all | solution.py:34
  56.8 7.6 %all-to-all-start.2 = ((bf16[16,64,384]{2,1,0:T(8,128)(2,1)}), bf16[16,64,384]{2,1,0:T(8,128)(2,1)S(1)}, u32[]{:S(2)}, u32[]{:S(2)}) async-start(bf16[16,64,384]{2,1,0:T(8,128)(2,1)} %pad_maximum_fusion), calls=%async_computation.2 | async-start | bytes 1572864 | tf_op jit(solution)/shard_map/all_to_all | solution.py:34
  64.4 3.0 %collective-permute-start.4 = (bf16[1024,128]{1,0:T(8,128)(2,1)}, bf16[1024,128]{1,0:T(8,128)(2,1)}, u32[]{:S(2)}, u32[]{:S(2)}) collective-permute-start(bf16[1024,128]{1,0:T(8,128)(2,1)} %copy-done.15), channel_id=1, source_target_pairs={{0,1},{1,0},{2,3},{3,2},{4,5},{5,4},{6,7},{7,6},{8,9},{9,8},{10,11... | collective-permute-start | bytes 786440 | tf_op jit(solution)/shard_map/ppermute | solution.py:48
  67.4 3.1 %collective-permute-start.5 = (bf16[1024,128]{1,0:T(8,128)(2,1)}, bf16[1024,128]{1,0:T(8,128)(2,1)}, u32[]{:S(2)}, u32[]{:S(2)}) collective-permute-start(bf16[1024,128]{1,0:T(8,128)(2,1)} %copy-done.12), channel_id=1, source_target_pairs={{0,2},{1,3},{2,0},{3,1},{4,6},{5,7},{6,4},{7,5},{8,10},{9,11},{10,... | collective-permute-start | bytes 786440 | tf_op jit(solution)/shard_map/ppermute | solution.py:48
  70.5 5.7 %collective-permute-start.6 = (bf16[1024,128]{1,0:T(8,128)(2,1)}, bf16[1024,128]{1,0:T(8,128)(2,1)}, u32[]{:S(2)}, u32[]{:S(2)}) collective-permute-start(bf16[1024,128]{1,0:T(8,128)(2,1)} %copy-done.11), channel_id=1, source_target_pairs={{0,4},{1,5},{2,6},{3,7},{4,0},{5,1},{6,2},{7,3},{8,12},{9,13},{10,... | collective-permute-start | bytes 786440 | tf_op jit(solution)/shard_map/ppermute | solution.py:48
  76.2 5.9 %collective-permute-start.7 = (bf16[1024,128]{1,0:T(8,128)(2,1)}, bf16[1024,128]{1,0:T(8,128)(2,1)}, u32[]{:S(2)}, u32[]{:S(2)}) collective-permute-start(bf16[1024,128]{1,0:T(8,128)(2,1)} %copy-done.10), channel_id=1, source_target_pairs={{0,8},{8,0},{1,9},{9,1},{2,10},{10,2},{3,11},{11,3},{4,12},{12,4},... | collective-permute-start | bytes 786440 | tf_op jit(solution)/shard_map/ppermute | solution.py:47
  82.4 9.5 %collective-permute-done.5.b = bf16[1024,128]{1,0:T(8,128)(2,1)} collective-permute-done((bf16[1024,128]{1,0:T(8,128)(2,1)}, bf16[1024,128]{1,0:T(8,128)(2,1)}, u32[]{:S(2)}, u32[]{:S(2)}) %collective-permute-start.5) | collective-permute-done | bytes 262176 | tf_op jit(solution)/shard_map/ppermute | solution.py:48
  92.0 2.6 %shard_map.104 = (bf16[1024,128]{1,0:T(8,128)(2,1)S(1)}, bf16[1024,256]{1,0:T(8,128)(2,1)}) custom-call(s32[1]{0:T(128)} %bitcast.1.core_ref, f32[1024,128]{1,0:T(8,128)S(1)} %shard_map.103.hidden_ref, bf16[1024,128]{1,0:T(8,128)(2,1)} %collective-permute-done.4.a, bf16[1024,128]{1,0:T(8,128)(2,1)} %collective-permute-done.5.b, ...), custom_call_target="tpu_custom_call" | custom-call | flops 67108864 | bytes 3538948 | tf_op jit(solution)/shard_map/pallas_call | solution.py:66
  94.6 9.9 %all-to-all-start.3 = ((bf16[32,32,256]{2,1,0:T(8,128)(2,1)}), bf16[32,32,256]{2,1,0:T(8,128)(2,1)}, u32[]{:S(2)}, u32[]{:S(2)}) async-start(bf16[32,32,256]{2,1,0:T(8,128)(2,1)} %bitcast.13), calls=%async_computation.3 | async-start | bytes 1048576 | tf_op jit(solution)/shard_map/all_to_all | solution.py:34
  104.5 3.4 %collective-permute-start.8 = (bf16[1024,128]{1,0:T(8,128)(2,1)S(1)}, bf16[1024,128]{1,0:T(8,128)(2,1)S(1)}, u32[]{:S(2)}, u32[]{:S(2)}) collective-permute-start(bf16[1024,128]{1,0:T(8,128)(2,1)S(1)} %get-tuple-element.73.a), channel_id=1, source_target_pairs={{0,1},{1,0},{2,3},{3,2},{4,5},{5,4},{6,7},{7,6},{8,9},{9,8},{10,11... | collective-permute-start | bytes 786440 | tf_op jit(solution)/shard_map/ppermute | solution.py:48
  107.9 4.3 %collective-permute-start.9 = (bf16[1024,128]{1,0:T(8,128)(2,1)S(1)}, bf16[1024,128]{1,0:T(8,128)(2,1)}, u32[]{:S(2)}, u32[]{:S(2)}) collective-permute-start(bf16[1024,128]{1,0:T(8,128)(2,1)S(1)} %get-tuple-element.73.a), channel_id=1, source_target_pairs={{0,2},{1,3},{2,0},{3,1},{4,6},{5,7},{6,4},{7,5},{8,10},{9,11},{10,... | collective-permute-start | bytes 786440 | tf_op jit(solution)/shard_map/ppermute | solution.py:48
  112.2 5.1 %collective-permute-start.10 = (bf16[1024,128]{1,0:T(8,128)(2,1)S(1)}, bf16[1024,128]{1,0:T(8,128)(2,1)}, u32[]{:S(2)}, u32[]{:S(2)}) collective-permute-start(bf16[1024,128]{1,0:T(8,128)(2,1)S(1)} %get-tuple-element.73.a), channel_id=1, source_target_pairs={{0,4},{1,5},{2,6},{3,7},{4,0},{5,1},{6,2},{7,3},{8,12},{9,13},{10,... | collective-permute-start | bytes 786440 | tf_op jit(solution)/shard_map/ppermute | solution.py:48
  117.3 7.3 %collective-permute-start.11 = (bf16[1024,128]{1,0:T(8,128)(2,1)S(1)}, bf16[1024,128]{1,0:T(8,128)(2,1)}, u32[]{:S(2)}, u32[]{:S(2)}) collective-permute-start(bf16[1024,128]{1,0:T(8,128)(2,1)S(1)} %get-tuple-element.73.a), channel_id=1, source_target_pairs={{0,8},{8,0},{1,9},{9,1},{2,10},{10,2},{3,11},{11,3},{4,12},{12,4},... | collective-permute-start | bytes 786440 | tf_op jit(solution)/shard_map/ppermute | solution.py:47
  125.7 13.2 %all_to_all.35 = bf16[8,32,256]{2,1,0:T(8,128)(2,1)S(1)} all-to-all(bf16[8,32,256]{2,1,0:T(8,128)(2,1)S(1)} %broadcast_in_dim.31), channel_id=1, replica_groups=mesh['x'=4,'y'=4,'c'=2,'h'=2,'z'=8] {'z'}, dimensions={0} | all-to-all | bytes 262144 | tf_op jit(solution)/shard_map/all_to_all | solution.py:34
  139.6 2.7 %shard_map.105 = (f32[256,512]{1,0:T(8,128)S(1)}, bf16[256,512]{1,0:T(8,128)(2,1)}, bf16[256,512]{1,0:T(8,128)(2,1)}, bf16[256,512]{1,0:T(8,128)(2,1)}) custom-call(s32[5]{0:T(128)S(1)} %select_reduce_fusion.slot_ref, s32[1]{0:T(128)} %bitcast.2.x_ref, bf16[1024,128]{1,0:T(8,128)(2,1)S(1)} %get-tuple-element.73.a, ...), custom_call_target="tpu_custom_call" | custom-call | flops 671088640 | bytes 3309592 | tf_op jit(solution)/shard_map/pallas_call | solution.py:66
  143.2 2.9 %collective-permute-start.14 = (bf16[256,512]{1,0:T(8,128)(2,1)}, bf16[256,512]{1,0:T(8,128)(2,1)S(1)}, u32[]{:S(2)}, u32[]{:S(2)}) collective-permute-start(bf16[256,512]{1,0:T(8,128)(2,1)} %get-tuple-element.70), channel_id=1, source_target_pairs={{0,384},{128,0},{256,128},{384,256},{1,385},{129,1},{257,129},{385... | collective-permute-start | bytes 786440 | tf_op jit(solution)/shard_map/ppermute | solution.py:52
  146.0 3.1 %collective-permute-start.13 = (bf16[256,512]{1,0:T(8,128)(2,1)}, bf16[256,512]{1,0:T(8,128)(2,1)S(1)}, u32[]{:S(2)}, u32[]{:S(2)}) collective-permute-start(bf16[256,512]{1,0:T(8,128)(2,1)} %get-tuple-element.69), channel_id=1, source_target_pairs={{0,256},{128,384},{256,0},{384,128},{1,257},{129,385},{257,1},{385... | collective-permute-start | bytes 786440 | tf_op jit(solution)/shard_map/ppermute | solution.py:52
  149.1 4.0 %collective-permute-start.12 = (bf16[256,512]{1,0:T(8,128)(2,1)}, bf16[256,512]{1,0:T(8,128)(2,1)}, u32[]{:S(2)}, u32[]{:S(2)}) collective-permute-start(bf16[256,512]{1,0:T(8,128)(2,1)} %get-tuple-element.68), channel_id=1, source_target_pairs={{0,128},{128,256},{256,384},{384,0},{1,129},{129,257},{257,385},{3... | collective-permute-start | bytes 786440 | tf_op jit(solution)/shard_map/ppermute | solution.py:52
  154.0 9.3 %all-to-all-start.5 = ((bf16[32,32,256]{2,1,0:T(8,128)(2,1)}), bf16[32,32,256]{2,1,0:T(8,128)(2,1)S(1)}, u32[]{:S(2)}, u32[]{:S(2)}) async-start(bf16[32,32,256]{2,1,0:T(8,128)(2,1)} %broadcast_in_dim.56), calls=%async_computation.5 | async-start | bytes 1048576 | tf_op jit(solution)/shard_map/all_to_all | solution.py:34
  165.0 2.9 %shard_map.106 = (f32[5,64,512]{2,1,0:T(8,128)S(1)}, f32[352,512]{1,0:T(8,128)}, f32[64,256]{1,0:T(8,128)S(1)}) custom-call(s32[5]{0:T(128)S(1)} %select_reduce_fusion.slot_ref, bf16[1024,128]{1,0:T(8,128)(2,1)S(1)} %copy-done.5, bf16[1024,128]{1,0:T(8,128)(2,1)S(1)} %copy-done.7, bf16[1024,128]{1,0:T(8,128)(2,1)} %collective-permute-done.9.c, ...), custom_call_target="tpu_custom_call" | custom-call | flops 738197504 | bytes 4587540 | tf_op jit(solution)/shard_map/pallas_call | solution.py:66
  168.6 1.9 %collective-permute-start.15 = (f32[352,512]{1,0:T(8,128)}, f32[352,512]{1,0:T(8,128)}, u32[]{:S(2)}, u32[]{:S(2)}) collective-permute-start(f32[352,512]{1,0:T(8,128)} %get-tuple-element.80), channel_id=1, source_target_pairs={{0,16},{16,0},{1,17},{17,1},{2,18},{18,2},{3,19},{19,3},{4,20},{20... | collective-permute-start | bytes 2162696 | tf_op jit(solution)/shard_map/ppermute | solution.py:42
  170.5 2.1 %convert_add_fusion = bf16[256,512]{1,0:T(8,128)(2,1)} fusion(bf16[256,512]{1,0:T(8,128)(2,1)} %copy-done.21, bf16[256,512]{1,0:T(8,128)(2,1)} %copy-done.22, f32[256,512]{1,0:T(8,128)} %copy-done.1, bf16[256,512]{1,0:T(8,128)(2,1)} %collective-permute-done.12), kind=kLoop, calls=%fused_computation.6 | loop fusion | flops 917504 | bytes 1572864 | tf_op jit(solution)/shard_map/add | solution.py:223
  175.7 4.0 %all-to-all-start.6 = ((bf16[4,64,512]{2,1,0:T(8,128)(2,1)}), bf16[4,64,512]{2,1,0:T(8,128)(2,1)S(1)}, u32[]{:S(2)}, u32[]{:S(2)}) async-start(bf16[4,64,512]{2,1,0:T(8,128)(2,1)} %bitcast.15), calls=%async_computation.6 | async-start | bytes 524288 | tf_op jit(solution)/shard_map/all_to_all | solution.py:34
  181.0 1.9 %collective-permute-start.16 = (f32[512,256]{1,0:T(8,128)S(1)}, f32[512,256]{1,0:T(8,128)S(1)}, u32[]{:S(2)}, u32[]{:S(2)}) collective-permute-start(f32[512,256]{1,0:T(8,128)S(1)} %shard_map.107), channel_id=1, source_target_pairs={{0,16},{16,0},{1,17},{17,1},{2,18},{18,2},{3,19},{19,3},{4,20},{20... | collective-permute-start | bytes 1572872 | tf_op jit(solution)/shard_map/ppermute | solution.py:42
  183.5 5.4 %all-to-all-done.6 = bf16[4,64,512]{2,1,0:T(8,128)(2,1)S(1)} async-done(((bf16[4,64,512]{2,1,0:T(8,128)(2,1)}), bf16[4,64,512]{2,1,0:T(8,128)(2,1)S(1)}, u32[]{:S(2)}, u32[]{:S(2)}) %all-to-all-start.6) | async-done | bytes 262176 | tf_op jit(solution)/shard_map/all_to_all | solution.py:34
  (96 shorter events, 26.8 us)
Async XLA Ops:
  0.6 30.8 %copy-start = (bf16[1,2048,64]{1,2,0:T(8,128)(2,1)S(1)}, bf16[1,2048,64]{1,2,0:T(8,128)(2,1)}, u32[]{:S(2)}) copy-start(bf16[1,2048,64]{1,2,0:T(8,128)(2,1)} %param.12) | copy-start | bytes 786436
  0.6 9.3 %copy-start.20 = (bf16[64,512]{1,0:T(8,128)(2,1)S(1)}, bf16[64,512]{1,0:T(8,128)(2,1)}, u32[]{:S(2)}) copy-start(bf16[64,512]{1,0:T(8,128)(2,1)} %param.7) | copy-start | bytes 196612
  0.7 9.2 %copy-start.18 = (bf16[512,256]{1,0:T(8,128)(2,1)S(1)}, bf16[512,256]{1,0:T(8,128)(2,1)}, u32[]{:S(2)}) copy-start(bf16[512,256]{1,0:T(8,128)(2,1)} %param.10) | copy-start | bytes 786436
  2.3 13.8 %all-to-all-start = ((bf16[4,64,512]{2,1,0:T(8,128)(2,1)}), bf16[4,64,512]{2,1,0:T(8,128)(2,1)S(1)}, u32[]{:S(2)}, u32[]{:S(2)}) async-start(bf16[4,64,512]{2,1,0:T(8,128)(2,1)} %broadcast_in_dim.28), calls=%async_computation | async-start | bytes 524288 | tf_op jit(solution)/shard_map/all_to_all | solution.py:34
  8.0 3.6 %collective-permute-start = (bf16[352,512]{1,0:T(8,128)(2,1)S(1)}, bf16[352,512]{1,0:T(8,128)(2,1)S(1)}, u32[]{:S(2)}, u32[]{:S(2)}) collective-permute-start(bf16[352,512]{1,0:T(8,128)(2,1)S(1)} %maximum_maximum_fusion), channel_id=1, source_target_pairs={{0,16},{16,0},{1,17},{17,1},{2,18},{18,2},{3,19},{19,3},{4,20},{20... | collective-permute-start | bytes 1081352 | tf_op jit(solution)/shard_map/ppermute | solution.py:42
  16.1 24.1 %copy-start.25 = (s32[5]{0:T(128)S(1)}, s32[5]{0:T(128)}, u32[]{:S(2)}) copy-start(s32[5]{0:T(128)} %constant.39.clone) | copy-start | bytes 64
  16.1 24.1 %copy-start.24 = (s32[1,5]{1,0:T(1,128)S(1)}, s32[1,5]{1,0:T(1,128)}, u32[]{:S(2)}) copy-start(s32[1,5]{1,0:T(1,128)} %param.9) | copy-start | bytes 64
  17.0 30.9 %all-to-all-start.1 = ((bf16[16,64,256]{2,1,0:T(8,128)(2,1)}), bf16[16,64,256]{2,1,0:T(8,128)(2,1)S(1)}, u32[]{:S(2)}, u32[]{:S(2)}) async-start(bf16[16,64,256]{2,1,0:T(8,128)(2,1)} %broadcast_in_dim.29), calls=%async_computation.1 | async-start | bytes 1048576 | tf_op jit(solution)/shard_map/all_to_all | solution.py:34
  31.5 17.6 %collective-permute-start.1 = (bf16[256,512]{1,0:T(8,128)(2,1)S(1)}, bf16[256,512]{1,0:T(8,128)(2,1)S(1)}, u32[]{:S(2)}, u32[]{:S(2)}) collective-permute-start(bf16[256,512]{1,0:T(8,128)(2,1)S(1)} %bitcast.44), channel_id=1, source_target_pairs={{0,128},{128,256},{256,384},{384,0},{1,129},{129,257},{257,385},{3... | collective-permute-start | bytes 786440 | tf_op jit(solution)/shard_map/ppermute | solution.py:52
  33.9 15.2 %collective-permute-start.2 = (bf16[256,512]{1,0:T(8,128)(2,1)S(1)}, bf16[256,512]{1,0:T(8,128)(2,1)S(1)}, u32[]{:S(2)}, u32[]{:S(2)}) collective-permute-start(bf16[256,512]{1,0:T(8,128)(2,1)S(1)} %bitcast.45), channel_id=1, source_target_pairs={{0,256},{128,384},{256,0},{384,128},{1,257},{129,385},{257,1},{385... | collective-permute-start | bytes 786440 | tf_op jit(solution)/shard_map/ppermute | solution.py:52
  38.3 11.6 %collective-permute-start.3 = (bf16[256,512]{1,0:T(8,128)(2,1)S(1)}, bf16[256,512]{1,0:T(8,128)(2,1)S(1)}, u32[]{:S(2)}, u32[]{:S(2)}) collective-permute-start(bf16[256,512]{1,0:T(8,128)(2,1)S(1)} %bitcast.46), channel_id=1, source_target_pairs={{0,384},{128,0},{256,128},{384,256},{1,385},{129,1},{257,129},{385... | collective-permute-start | bytes 786440 | tf_op jit(solution)/shard_map/ppermute | solution.py:52
  56.1 26.0 %copy-start.3 = (bf16[256,1,64]{0,2,1:T(8,128)(2,1)S(1)}, bf16[256,1,64]{0,2,1:T(8,128)(2,1)}, u32[]{:S(2)}) copy-start(bf16[256,1,64]{0,2,1:T(8,128)(2,1)} %param.11) | copy-start | bytes 98308
  56.8 25.3 %all-to-all-start.2 = ((bf16[16,64,384]{2,1,0:T(8,128)(2,1)}), bf16[16,64,384]{2,1,0:T(8,128)(2,1)S(1)}, u32[]{:S(2)}, u32[]{:S(2)}) async-start(bf16[16,64,384]{2,1,0:T(8,128)(2,1)} %pad_maximum_fusion), calls=%async_computation.2 | async-start | bytes 1572864 | tf_op jit(solution)/shard_map/all_to_all | solution.py:34
  64.4 18.1 %collective-permute-start.4 = (bf16[1024,128]{1,0:T(8,128)(2,1)}, bf16[1024,128]{1,0:T(8,128)(2,1)}, u32[]{:S(2)}, u32[]{:S(2)}) collective-permute-start(bf16[1024,128]{1,0:T(8,128)(2,1)} %copy-done.15), channel_id=1, source_target_pairs={{0,1},{1,0},{2,3},{3,2},{4,5},{5,4},{6,7},{7,6},{8,9},{9,8},{10,11... | collective-permute-start | bytes 786440 | tf_op jit(solution)/shard_map/ppermute | solution.py:48
  67.4 24.6 %collective-permute-start.5 = (bf16[1024,128]{1,0:T(8,128)(2,1)}, bf16[1024,128]{1,0:T(8,128)(2,1)}, u32[]{:S(2)}, u32[]{:S(2)}) collective-permute-start(bf16[1024,128]{1,0:T(8,128)(2,1)} %copy-done.12), channel_id=1, source_target_pairs={{0,2},{1,3},{2,0},{3,1},{4,6},{5,7},{6,4},{7,5},{8,10},{9,11},{10,... | collective-permute-start | bytes 786440 | tf_op jit(solution)/shard_map/ppermute | solution.py:48
  70.5 21.5 %collective-permute-start.6 = (bf16[1024,128]{1,0:T(8,128)(2,1)}, bf16[1024,128]{1,0:T(8,128)(2,1)}, u32[]{:S(2)}, u32[]{:S(2)}) collective-permute-start(bf16[1024,128]{1,0:T(8,128)(2,1)} %copy-done.11), channel_id=1, source_target_pairs={{0,4},{1,5},{2,6},{3,7},{4,0},{5,1},{6,2},{7,3},{8,12},{9,13},{10,... | collective-permute-start | bytes 786440 | tf_op jit(solution)/shard_map/ppermute | solution.py:48
  76.2 15.8 %collective-permute-start.7 = (bf16[1024,128]{1,0:T(8,128)(2,1)}, bf16[1024,128]{1,0:T(8,128)(2,1)}, u32[]{:S(2)}, u32[]{:S(2)}) collective-permute-start(bf16[1024,128]{1,0:T(8,128)(2,1)} %copy-done.10), channel_id=1, source_target_pairs={{0,8},{8,0},{1,9},{9,1},{2,10},{10,2},{3,11},{11,3},{4,12},{12,4},... | collective-permute-start | bytes 786440 | tf_op jit(solution)/shard_map/ppermute | solution.py:47
  94.6 45.1 %copy-start.4 = (bf16[1024,128]{1,0:T(8,128)(2,1)}, bf16[1024,128]{1,0:T(8,128)(2,1)S(1)}, u32[]{:S(2)}) copy-start(bf16[1024,128]{1,0:T(8,128)(2,1)S(1)} %get-tuple-element.73.a) | copy-start | bytes 786436
  94.6 30.0 %all-to-all-start.3 = ((bf16[32,32,256]{2,1,0:T(8,128)(2,1)}), bf16[32,32,256]{2,1,0:T(8,128)(2,1)}, u32[]{:S(2)}, u32[]{:S(2)}) async-start(bf16[32,32,256]{2,1,0:T(8,128)(2,1)} %bitcast.13), calls=%async_computation.3 | async-start | bytes 1048576 | tf_op jit(solution)/shard_map/all_to_all | solution.py:34
  104.5 35.1 %collective-permute-start.8 = (bf16[1024,128]{1,0:T(8,128)(2,1)S(1)}, bf16[1024,128]{1,0:T(8,128)(2,1)S(1)}, u32[]{:S(2)}, u32[]{:S(2)}) collective-permute-start(bf16[1024,128]{1,0:T(8,128)(2,1)S(1)} %get-tuple-element.73.a), channel_id=1, source_target_pairs={{0,1},{1,0},{2,3},{3,2},{4,5},{5,4},{6,7},{7,6},{8,9},{9,8},{10,11... | collective-permute-start | bytes 786440 | tf_op jit(solution)/shard_map/ppermute | solution.py:48
  107.9 31.7 %collective-permute-start.9 = (bf16[1024,128]{1,0:T(8,128)(2,1)S(1)}, bf16[1024,128]{1,0:T(8,128)(2,1)}, u32[]{:S(2)}, u32[]{:S(2)}) collective-permute-start(bf16[1024,128]{1,0:T(8,128)(2,1)S(1)} %get-tuple-element.73.a), channel_id=1, source_target_pairs={{0,2},{1,3},{2,0},{3,1},{4,6},{5,7},{6,4},{7,5},{8,10},{9,11},{10,... | collective-permute-start | bytes 786440 | tf_op jit(solution)/shard_map/ppermute | solution.py:48
  112.2 27.4 %collective-permute-start.10 = (bf16[1024,128]{1,0:T(8,128)(2,1)S(1)}, bf16[1024,128]{1,0:T(8,128)(2,1)}, u32[]{:S(2)}, u32[]{:S(2)}) collective-permute-start(bf16[1024,128]{1,0:T(8,128)(2,1)S(1)} %get-tuple-element.73.a), channel_id=1, source_target_pairs={{0,4},{1,5},{2,6},{3,7},{4,0},{5,1},{6,2},{7,3},{8,12},{9,13},{10,... | collective-permute-start | bytes 786440 | tf_op jit(solution)/shard_map/ppermute | solution.py:48
  117.3 22.3 %collective-permute-start.11 = (bf16[1024,128]{1,0:T(8,128)(2,1)S(1)}, bf16[1024,128]{1,0:T(8,128)(2,1)}, u32[]{:S(2)}, u32[]{:S(2)}) collective-permute-start(bf16[1024,128]{1,0:T(8,128)(2,1)S(1)} %get-tuple-element.73.a), channel_id=1, source_target_pairs={{0,8},{8,0},{1,9},{9,1},{2,10},{10,2},{3,11},{11,3},{4,12},{12,4},... | collective-permute-start | bytes 786440 | tf_op jit(solution)/shard_map/ppermute | solution.py:47
  139.6 13.5 %copy-start.23 = (bf16[32,256]{1,0:T(8,128)(2,1)S(1)}, bf16[32,256]{1,0:T(8,128)(2,1)}, u32[]{:S(2)}) copy-start(bf16[32,256]{1,0:T(8,128)(2,1)} %reduce_sum.57) | copy-start | bytes 49156
  143.2 20.9 %copy-start.5 = (bf16[1024,128]{1,0:T(8,128)(2,1)S(1)}, bf16[1024,128]{1,0:T(8,128)(2,1)}, u32[]{:S(2)}) copy-start(bf16[1024,128]{1,0:T(8,128)(2,1)} %copy-done.4) | copy-start | bytes 786436
  143.2 20.1 %collective-permute-start.14 = (bf16[256,512]{1,0:T(8,128)(2,1)}, bf16[256,512]{1,0:T(8,128)(2,1)S(1)}, u32[]{:S(2)}, u32[]{:S(2)}) collective-permute-start(bf16[256,512]{1,0:T(8,128)(2,1)} %get-tuple-element.70), channel_id=1, source_target_pairs={{0,384},{128,0},{256,128},{384,256},{1,385},{129,1},{257,129},{385... | collective-permute-start | bytes 786440 | tf_op jit(solution)/shard_map/ppermute | solution.py:52
  146.0 17.3 %collective-permute-start.13 = (bf16[256,512]{1,0:T(8,128)(2,1)}, bf16[256,512]{1,0:T(8,128)(2,1)S(1)}, u32[]{:S(2)}, u32[]{:S(2)}) collective-permute-start(bf16[256,512]{1,0:T(8,128)(2,1)} %get-tuple-element.69), channel_id=1, source_target_pairs={{0,256},{128,384},{256,0},{384,128},{1,257},{129,385},{257,1},{385... | collective-permute-start | bytes 786440 | tf_op jit(solution)/shard_map/ppermute | solution.py:52
  149.1 14.2 %collective-permute-start.12 = (bf16[256,512]{1,0:T(8,128)(2,1)}, bf16[256,512]{1,0:T(8,128)(2,1)}, u32[]{:S(2)}, u32[]{:S(2)}) collective-permute-start(bf16[256,512]{1,0:T(8,128)(2,1)} %get-tuple-element.68), channel_id=1, source_target_pairs={{0,128},{128,256},{256,384},{384,0},{1,129},{129,257},{257,385},{3... | collective-permute-start | bytes 786440 | tf_op jit(solution)/shard_map/ppermute | solution.py:52
  154.0 21.8 %all-to-all-start.5 = ((bf16[32,32,256]{2,1,0:T(8,128)(2,1)}), bf16[32,32,256]{2,1,0:T(8,128)(2,1)S(1)}, u32[]{:S(2)}, u32[]{:S(2)}) async-start(bf16[32,32,256]{2,1,0:T(8,128)(2,1)} %broadcast_in_dim.56), calls=%async_computation.5 | async-start | bytes 1048576 | tf_op jit(solution)/shard_map/all_to_all | solution.py:34
  168.6 4.4 %collective-permute-start.15 = (f32[352,512]{1,0:T(8,128)}, f32[352,512]{1,0:T(8,128)}, u32[]{:S(2)}, u32[]{:S(2)}) collective-permute-start(f32[352,512]{1,0:T(8,128)} %get-tuple-element.80), channel_id=1, source_target_pairs={{0,16},{16,0},{1,17},{17,1},{2,18},{18,2},{3,19},{19,3},{4,20},{20... | collective-permute-start | bytes 2162696 | tf_op jit(solution)/shard_map/ppermute | solution.py:42
  175.7 13.2 %all-to-all-start.6 = ((bf16[4,64,512]{2,1,0:T(8,128)(2,1)}), bf16[4,64,512]{2,1,0:T(8,128)(2,1)S(1)}, u32[]{:S(2)}, u32[]{:S(2)}) async-start(bf16[4,64,512]{2,1,0:T(8,128)(2,1)} %bitcast.15), calls=%async_computation.6 | async-start | bytes 524288 | tf_op jit(solution)/shard_map/all_to_all | solution.py:34
  181.0 8.8 %collective-permute-start.16 = (f32[512,256]{1,0:T(8,128)S(1)}, f32[512,256]{1,0:T(8,128)S(1)}, u32[]{:S(2)}, u32[]{:S(2)}) collective-permute-start(f32[512,256]{1,0:T(8,128)S(1)} %shard_map.107), channel_id=1, source_target_pairs={{0,16},{16,0},{1,17},{17,1},{2,18},{18,2},{3,19},{19,3},{4,20},{20... | collective-permute-start | bytes 1572872 | tf_op jit(solution)/shard_map/ppermute | solution.py:42
  (17 other events, 31.0 us)

commit v4 on v3

--- a/solution.py
+++ b/solution.py
@@ -95,15 +95,19 @@
     return pl.ds(pl.multiple_of(lax.rem(x + shift, X) * STEP, STEP), STEP)
 
 
-def forward_kernel(slot_ref, x_ref, t0, t1, t2, t3, mine_ref, other_ref, tile_ref, *outs):
+def forward_kernel(slot_ref, x_ref, t0, t1, t2, t3, mine_ref, other_ref, *outs):
     weights = all_weights(slot_ref, mine_ref, other_ref)
     for shift, part in enumerate((t0, t1, t2, t3)):
         rows = place_of(x_ref[0], X - shift)
-        tile_ref[rows, :] = part[...]
         products = dot(part[...], weights, 1, 1)
         outs[0][rows, :] = products[:, :COLS]
         for kind in range(1, SLOTS):
             outs[kind][rows, :] = products[:, kind * COLS : (kind + 1) * COLS].astype(BF16)
+
+
+def tile_kernel(x_ref, t0, t1, t2, t3, tile_ref):
+    for shift, part in enumerate((t0, t1, t2, t3)):
+        tile_ref[place_of(x_ref[0], X - shift), :] = part[...]
 
 
 def low_kernel(hidden_ref, sent_ref, factor_ref, other_ref, out_ref):
@@ -183,9 +187,9 @@
     near = after(near, codes)
 
     tall = [shape((TOKENS, COLS), BF16)] * 4
-    tile, hidden, *terms = call(
+    hidden, *terms = call(
         forward_kernel, [SMEM] * 2 + [VMEM] * 6,
-        [shape((TOKENS, ROWS), BF16), shape((TOKENS, COLS), F32)] + tall,
+        [shape((TOKENS, COLS), F32)] + tall,
         2 * TOKENS * COLS * SLOTS * ROWS, slots, place, near, *far, mine, other,
     )
     arrived = [from_partner(term, mask) for term, mask in zip(terms, MASKS[1:])]
@@ -219,6 +223,10 @@
     )
     came = [to_x(part, shift) for shift, part in enumerate(away, 1)]
     kinds = lax.optimization_barrier((*kinds, *came))[:SLOTS]
+    near, *far = lax.optimization_barrier((near, *far, *came))[:X]
+    (tile,) = call(
+        tile_kernel, [SMEM] + [VMEM] * 4, [shape((TOKENS, ROWS), BF16)], 0, place, near, *far
+    )
     for part in came:
         partial = partial + part.astype(F32)
     partial = after(partial, back)

time: 192 us -> 191 us (level)
    unnamed x52 -> x46, local copies, waits for them, and re-layouts: 9.32 us -> 8.26 us
    pallas_call x6 -> x7, Pallas kernels: 10.6 us -> 10.5 us  [call(): pl.pallas_call(kernel, out_shape=outs, in_specs=ins, out_specs=[VMEM] * l...]
where the time goes in v4:
time: 191 us; the launch traced here: 190 us
  starting transfers between devices  113 us (59%)
  waiting for transfers between devices  29.1 us (15%)
  local copies, waits for them, and re-layouts  14.4 us (8%)
  blocking collectives  13.2 us (7%)
  Pallas kernels  10.5 us (5%)
  other arithmetic  7.05 us (4%)
    all_to_all x6, starting transfers between devices, exchange(): return lax.all_to_all(block, axes, 0, 0, tiled=True)  50.5 us
    ppermute x6, starting transfers between devices, from_partner(): return lax.ppermute(block, 'z', [(k, k ^ mask) for k in range(Z)])  24.6 us
    ppermute x6, starting transfers between devices, to_x(): return lax.ppermute(block, 'x', [(k, (k + shift) % X) for k in range(X)])  18.4 us
    all_to_all x6, waiting for transfers between devices, exchange(): return lax.all_to_all(block, axes, 0, 0, tiled=True)  17.5 us
    ppermute x2, starting transfers between devices, from_partner(): return lax.ppermute(block, 'h', [(0, 1), (1, 0)])  13.9 us
    all_to_all x1, blocking collectives, exchange(): return lax.all_to_all(block, axes, 0, 0, tiled=True)  13.2 us
    pallas_call x7, Pallas kernels, call(): pl.pallas_call(kernel, out_shape=outs, in_specs=ins, out_specs=[VMEM] * l...  10.5 us
    ppermute x6, waiting for transfers between devices, from_partner(): return lax.ppermute(block, 'z', [(k, k ^ mask) for k in range(Z)])  9.57 us
  transfers between devices with their start and end apart: 23, of which 7 were waited for; matrix products, arithmetic and copies ran while one was open for 6% of the time, Pallas kernels for 2%

profile of v4, /device:TPU:6, one launch (start us, length us, event | category | flops | bytes accessed | tf_op | source)
XLA Modules:
  0.0 189.5 jit_solution(3391041039712361601)
XLA Ops:
  2.3 4.9 %all-to-all-start = ((bf16[4,64,512]{2,1,0:T(8,128)(2,1)}), bf16[4,64,512]{2,1,0:T(8,128)(2,1)S(1)}, u32[]{:S(2)}, u32[]{:S(2)}) async-start(bf16[4,64,512]{2,1,0:T(8,128)(2,1)} %broadcast_in_dim.28), calls=%async_computation | async-start | bytes 524288 | tf_op jit(solution)/shard_map/all_to_all | solution.py:34
  8.0 1.9 %collective-permute-start = (bf16[352,512]{1,0:T(8,128)(2,1)S(1)}, bf16[352,512]{1,0:T(8,128)(2,1)S(1)}, u32[]{:S(2)}, u32[]{:S(2)}) collective-permute-start(bf16[352,512]{1,0:T(8,128)(2,1)S(1)} %maximum_maximum_fusion), channel_id=1, source_target_pairs={{0,16},{16,0},{1,17},{17,1},{2,18},{18,2},{3,19},{19,3},{4,20},{20... | collective-permute-start | bytes 1081352 | tf_op jit(solution)/shard_map/ppermute | solution.py:42
  11.5 4.6 %all-to-all-done = bf16[4,64,512]{2,1,0:T(8,128)(2,1)S(1)} async-done(((bf16[4,64,512]{2,1,0:T(8,128)(2,1)}), bf16[4,64,512]{2,1,0:T(8,128)(2,1)S(1)}, u32[]{:S(2)}, u32[]{:S(2)}) %all-to-all-start) | async-done | bytes 262176 | tf_op jit(solution)/shard_map/all_to_all | solution.py:34
  17.0 14.5 %all-to-all-start.1 = ((bf16[16,64,256]{2,1,0:T(8,128)(2,1)}), bf16[16,64,256]{2,1,0:T(8,128)(2,1)S(1)}, u32[]{:S(2)}, u32[]{:S(2)}) async-start(bf16[16,64,256]{2,1,0:T(8,128)(2,1)} %broadcast_in_dim.29), calls=%async_computation.1 | async-start | bytes 1048576 | tf_op jit(solution)/shard_map/all_to_all | solution.py:34
  31.5 2.4 %collective-permute-start.1 = (bf16[256,512]{1,0:T(8,128)(2,1)S(1)}, bf16[256,512]{1,0:T(8,128)(2,1)S(1)}, u32[]{:S(2)}, u32[]{:S(2)}) collective-permute-start(bf16[256,512]{1,0:T(8,128)(2,1)S(1)} %bitcast.38), channel_id=1, source_target_pairs={{0,128},{128,256},{256,384},{384,0},{1,129},{129,257},{257,385},{3... | collective-permute-start | bytes 786440 | tf_op jit(solution)/shard_map/ppermute | solution.py:52
  33.9 4.3 %collective-permute-start.2 = (bf16[256,512]{1,0:T(8,128)(2,1)S(1)}, bf16[256,512]{1,0:T(8,128)(2,1)S(1)}, u32[]{:S(2)}, u32[]{:S(2)}) collective-permute-start(bf16[256,512]{1,0:T(8,128)(2,1)S(1)} %bitcast.39), channel_id=1, source_target_pairs={{0,256},{128,384},{256,0},{384,128},{1,257},{129,385},{257,1},{385... | collective-permute-start | bytes 786440 | tf_op jit(solution)/shard_map/ppermute | solution.py:52
  38.3 1.9 %collective-permute-start.3 = (bf16[256,512]{1,0:T(8,128)(2,1)S(1)}, bf16[256,512]{1,0:T(8,128)(2,1)S(1)}, u32[]{:S(2)}, u32[]{:S(2)}) collective-permute-start(bf16[256,512]{1,0:T(8,128)(2,1)S(1)} %bitcast.40), channel_id=1, source_target_pairs={{0,384},{128,0},{256,128},{384,256},{1,385},{129,1},{257,129},{385... | collective-permute-start | bytes 786440 | tf_op jit(solution)/shard_map/ppermute | solution.py:52
  40.4 7.5 %all-to-all-done.1 = bf16[16,64,256]{2,1,0:T(8,128)(2,1)S(1)} async-done(((bf16[16,64,256]{2,1,0:T(8,128)(2,1)}), bf16[16,64,256]{2,1,0:T(8,128)(2,1)S(1)}, u32[]{:S(2)}, u32[]{:S(2)}) %all-to-all-start.1) | async-done | bytes 524320 | tf_op jit(solution)/shard_map/all_to_all | solution.py:34
  53.1 7.3 %all-to-all-start.2 = ((bf16[16,64,384]{2,1,0:T(8,128)(2,1)}), bf16[16,64,384]{2,1,0:T(8,128)(2,1)S(1)}, u32[]{:S(2)}, u32[]{:S(2)}) async-start(bf16[16,64,384]{2,1,0:T(8,128)(2,1)} %pad_maximum_fusion), calls=%async_computation.2 | async-start | bytes 1572864 | tf_op jit(solution)/shard_map/all_to_all | solution.py:34
  60.5 3.0 %collective-permute-start.4 = (bf16[1024,128]{1,0:T(8,128)(2,1)}, bf16[1024,128]{1,0:T(8,128)(2,1)S(1)}, u32[]{:S(2)}, u32[]{:S(2)}) collective-permute-start(bf16[1024,128]{1,0:T(8,128)(2,1)} %copy-done.15), channel_id=1, source_target_pairs={{0,1},{1,0},{2,3},{3,2},{4,5},{5,4},{6,7},{7,6},{8,9},{9,8},{10,11... | collective-permute-start | bytes 786440 | tf_op jit(solution)/shard_map/ppermute | solution.py:48
  63.5 3.6 %collective-permute-start.5 = (bf16[1024,128]{1,0:T(8,128)(2,1)}, bf16[1024,128]{1,0:T(8,128)(2,1)}, u32[]{:S(2)}, u32[]{:S(2)}) collective-permute-start(bf16[1024,128]{1,0:T(8,128)(2,1)} %copy-done.14), channel_id=1, source_target_pairs={{0,2},{1,3},{2,0},{3,1},{4,6},{5,7},{6,4},{7,5},{8,10},{9,11},{10,... | collective-permute-start | bytes 786440 | tf_op jit(solution)/shard_map/ppermute | solution.py:48
  67.1 5.3 %collective-permute-start.6 = (bf16[1024,128]{1,0:T(8,128)(2,1)}, bf16[1024,128]{1,0:T(8,128)(2,1)}, u32[]{:S(2)}, u32[]{:S(2)}) collective-permute-start(bf16[1024,128]{1,0:T(8,128)(2,1)} %copy-done.13), channel_id=1, source_target_pairs={{0,4},{1,5},{2,6},{3,7},{4,0},{5,1},{6,2},{7,3},{8,12},{9,13},{10,... | collective-permute-start | bytes 786440 | tf_op jit(solution)/shard_map/ppermute | solution.py:48
  72.3 6.6 %collective-permute-start.7 = (bf16[1024,128]{1,0:T(8,128)(2,1)}, bf16[1024,128]{1,0:T(8,128)(2,1)}, u32[]{:S(2)}, u32[]{:S(2)}) collective-permute-start(bf16[1024,128]{1,0:T(8,128)(2,1)} %copy-done.12), channel_id=1, source_target_pairs={{0,8},{8,0},{1,9},{9,1},{2,10},{10,2},{3,11},{11,3},{4,12},{12,4},... | collective-permute-start | bytes 786440 | tf_op jit(solution)/shard_map/ppermute | solution.py:47
  79.3 9.6 %collective-permute-done.5.b = bf16[1024,128]{1,0:T(8,128)(2,1)} collective-permute-done((bf16[1024,128]{1,0:T(8,128)(2,1)}, bf16[1024,128]{1,0:T(8,128)(2,1)}, u32[]{:S(2)}, u32[]{:S(2)}) %collective-permute-start.5) | collective-permute-done | bytes 262176 | tf_op jit(solution)/shard_map/ppermute | solution.py:48
  88.8 2.5 %shard_map.104 = (bf16[1024,128]{1,0:T(8,128)(2,1)S(1)}, bf16[1024,256]{1,0:T(8,128)(2,1)}) custom-call(s32[1]{0:T(128)} %bitcast.1.core_ref, f32[1024,128]{1,0:T(8,128)S(1)} %shard_map.103.hidden_ref, bf16[1024,128]{1,0:T(8,128)(2,1)S(1)} %collective-permute-done.4.a, bf16[1024,128]{1,0:T(8,128)(2,1)} %collective-permute-done.5.b, ...), custom_call_target="tpu_custom_call" | custom-call | flops 67108864 | bytes 3538948 | tf_op jit(solution)/shard_map/pallas_call | solution.py:66
  91.3 9.9 %all-to-all-start.3 = ((bf16[32,32,256]{2,1,0:T(8,128)(2,1)}), bf16[32,32,256]{2,1,0:T(8,128)(2,1)}, u32[]{:S(2)}, u32[]{:S(2)}) async-start(bf16[32,32,256]{2,1,0:T(8,128)(2,1)} %bitcast.13), calls=%async_computation.3 | async-start | bytes 1048576 | tf_op jit(solution)/shard_map/all_to_all | solution.py:34
  101.3 3.4 %collective-permute-start.8 = (bf16[1024,128]{1,0:T(8,128)(2,1)S(1)}, bf16[1024,128]{1,0:T(8,128)(2,1)S(1)}, u32[]{:S(2)}, u32[]{:S(2)}) collective-permute-start(bf16[1024,128]{1,0:T(8,128)(2,1)S(1)} %get-tuple-element.76.a), channel_id=1, source_target_pairs={{0,1},{1,0},{2,3},{3,2},{4,5},{5,4},{6,7},{7,6},{8,9},{9,8},{10,11... | collective-permute-start | bytes 786440 | tf_op jit(solution)/shard_map/ppermute | solution.py:48
  104.6 4.3 %collective-permute-start.9 = (bf16[1024,128]{1,0:T(8,128)(2,1)S(1)}, bf16[1024,128]{1,0:T(8,128)(2,1)S(1)}, u32[]{:S(2)}, u32[]{:S(2)}) collective-permute-start(bf16[1024,128]{1,0:T(8,128)(2,1)S(1)} %get-tuple-element.76.a), channel_id=1, source_target_pairs={{0,2},{1,3},{2,0},{3,1},{4,6},{5,7},{6,4},{7,5},{8,10},{9,11},{10,... | collective-permute-start | bytes 786440 | tf_op jit(solution)/shard_map/ppermute | solution.py:48
  108.9 5.1 %collective-permute-start.10 = (bf16[1024,128]{1,0:T(8,128)(2,1)S(1)}, bf16[1024,128]{1,0:T(8,128)(2,1)}, u32[]{:S(2)}, u32[]{:S(2)}) collective-permute-start(bf16[1024,128]{1,0:T(8,128)(2,1)S(1)} %get-tuple-element.76.a), channel_id=1, source_target_pairs={{0,4},{1,5},{2,6},{3,7},{4,0},{5,1},{6,2},{7,3},{8,12},{9,13},{10,... | collective-permute-start | bytes 786440 | tf_op jit(solution)/shard_map/ppermute | solution.py:48
  114.0 7.3 %collective-permute-start.11 = (bf16[1024,128]{1,0:T(8,128)(2,1)S(1)}, bf16[1024,128]{1,0:T(8,128)(2,1)}, u32[]{:S(2)}, u32[]{:S(2)}) collective-permute-start(bf16[1024,128]{1,0:T(8,128)(2,1)S(1)} %get-tuple-element.76.a), channel_id=1, source_target_pairs={{0,8},{8,0},{1,9},{9,1},{2,10},{10,2},{3,11},{11,3},{4,12},{12,4},... | collective-permute-start | bytes 786440 | tf_op jit(solution)/shard_map/ppermute | solution.py:47
  122.5 13.2 %all_to_all.35 = bf16[8,32,256]{2,1,0:T(8,128)(2,1)S(1)} all-to-all(bf16[8,32,256]{2,1,0:T(8,128)(2,1)S(1)} %broadcast_in_dim.31), channel_id=1, replica_groups=mesh['x'=4,'y'=4,'c'=2,'h'=2,'z'=8] {'z'}, dimensions={0} | all-to-all | bytes 262144 | tf_op jit(solution)/shard_map/all_to_all | solution.py:34
  135.8 2.7 %shard_map.105 = (f32[256,512]{1,0:T(8,128)S(1)}, bf16[256,512]{1,0:T(8,128)(2,1)}, bf16[256,512]{1,0:T(8,128)(2,1)}, bf16[256,512]{1,0:T(8,128)(2,1)}) custom-call(s32[5]{0:T(128)S(1)} %select_reduce_fusion.slot_ref, s32[1]{0:T(128)} %bitcast.2.x_ref, bf16[1024,128]{1,0:T(8,128)(2,1)S(1)} %get-tuple-element.76.a, ...), custom_call_target="tpu_custom_call" | custom-call | flops 671088640 | bytes 3309592 | tf_op jit(solution)/shard_map/pallas_call | solution.py:66
  139.3 2.7 %collective-permute-start.14 = (bf16[256,512]{1,0:T(8,128)(2,1)}, bf16[256,512]{1,0:T(8,128)(2,1)S(1)}, u32[]{:S(2)}, u32[]{:S(2)}) collective-permute-start(bf16[256,512]{1,0:T(8,128)(2,1)} %get-tuple-element.73), channel_id=1, source_target_pairs={{0,384},{128,0},{256,128},{384,256},{1,385},{129,1},{257,129},{385... | collective-permute-start | bytes 786440 | tf_op jit(solution)/shard_map/ppermute | solution.py:52
  142.1 3.1 %collective-permute-start.13 = (bf16[256,512]{1,0:T(8,128)(2,1)}, bf16[256,512]{1,0:T(8,128)(2,1)S(1)}, u32[]{:S(2)}, u32[]{:S(2)}) collective-permute-start(bf16[256,512]{1,0:T(8,128)(2,1)} %get-tuple-element.72), channel_id=1, source_target_pairs={{0,256},{128,384},{256,0},{384,128},{1,257},{129,385},{257,1},{385... | collective-permute-start | bytes 786440 | tf_op jit(solution)/shard_map/ppermute | solution.py:52
  145.1 4.0 %collective-permute-start.12 = (bf16[256,512]{1,0:T(8,128)(2,1)}, bf16[256,512]{1,0:T(8,128)(2,1)}, u32[]{:S(2)}, u32[]{:S(2)}) collective-permute-start(bf16[256,512]{1,0:T(8,128)(2,1)} %get-tuple-element.71), channel_id=1, source_target_pairs={{0,128},{128,256},{256,384},{384,0},{1,129},{129,257},{257,385},{3... | collective-permute-start | bytes 786440 | tf_op jit(solution)/shard_map/ppermute | solution.py:52
  150.0 9.3 %all-to-all-start.5 = ((bf16[32,32,256]{2,1,0:T(8,128)(2,1)}), bf16[32,32,256]{2,1,0:T(8,128)(2,1)S(1)}, u32[]{:S(2)}, u32[]{:S(2)}) async-start(bf16[32,32,256]{2,1,0:T(8,128)(2,1)} %broadcast_in_dim.56), calls=%async_computation.5 | async-start | bytes 1048576 | tf_op jit(solution)/shard_map/all_to_all | solution.py:34
  164.6 2.9 %shard_map.107 = (f32[5,64,512]{2,1,0:T(8,128)S(1)}, f32[352,512]{1,0:T(8,128)}, f32[64,256]{1,0:T(8,128)S(1)}) custom-call(s32[5]{0:T(128)S(1)} %select_reduce_fusion.slot_ref, bf16[1024,128]{1,0:T(8,128)(2,1)S(1)} %copy-done.7, bf16[1024,128]{1,0:T(8,128)(2,1)S(1)} %copy-done.9, bf16[1024,128]{1,0:T(8,128)(2,1)S(1)} %copy-done.11, ...), custom_call_target="tpu_custom_call" | custom-call | flops 738197504 | bytes 4587540 | tf_op jit(solution)/shard_map/pallas_call | solution.py:66
  167.5 1.9 %collective-permute-start.15 = (f32[352,512]{1,0:T(8,128)}, f32[352,512]{1,0:T(8,128)}, u32[]{:S(2)}, u32[]{:S(2)}) collective-permute-start(f32[352,512]{1,0:T(8,128)} %get-tuple-element.86), channel_id=1, source_target_pairs={{0,16},{16,0},{1,17},{17,1},{2,18},{18,2},{3,19},{19,3},{4,20},{20... | collective-permute-start | bytes 2162696 | tf_op jit(solution)/shard_map/ppermute | solution.py:42
  169.4 2.1 %convert_add_fusion = bf16[256,512]{1,0:T(8,128)(2,1)} fusion(bf16[256,512]{1,0:T(8,128)(2,1)} %copy-done.19, bf16[256,512]{1,0:T(8,128)(2,1)} %copy-done.20, f32[256,512]{1,0:T(8,128)} %copy-done.1, bf16[256,512]{1,0:T(8,128)(2,1)} %collective-permute-done.12), kind=kLoop, calls=%fused_computation.6 | loop fusion | flops 917504 | bytes 1572864 | tf_op jit(solution)/shard_map/add | solution.py:231
  174.0 4.6 %all-to-all-start.6 = ((bf16[4,64,512]{2,1,0:T(8,128)(2,1)}), bf16[4,64,512]{2,1,0:T(8,128)(2,1)S(1)}, u32[]{:S(2)}, u32[]{:S(2)}) async-start(bf16[4,64,512]{2,1,0:T(8,128)(2,1)} %bitcast.50), calls=%async_computation.6 | async-start | bytes 524288 | tf_op jit(solution)/shard_map/all_to_all | solution.py:34
  179.8 1.9 %collective-permute-start.16 = (f32[512,256]{1,0:T(8,128)S(1)}, f32[512,256]{1,0:T(8,128)S(1)}, u32[]{:S(2)}, u32[]{:S(2)}) collective-permute-start(f32[512,256]{1,0:T(8,128)S(1)} %shard_map.108), channel_id=1, source_target_pairs={{0,16},{16,0},{1,17},{17,1},{2,18},{18,2},{3,19},{19,3},{4,20},{20... | collective-permute-start | bytes 1572872 | tf_op jit(solution)/shard_map/ppermute | solution.py:42
  182.4 5.4 %all-to-all-done.6 = bf16[4,64,512]{2,1,0:T(8,128)(2,1)S(1)} async-done(((bf16[4,64,512]{2,1,0:T(8,128)(2,1)}), bf16[4,64,512]{2,1,0:T(8,128)(2,1)S(1)}, u32[]{:S(2)}, u32[]{:S(2)}) %all-to-all-start.6) | async-done | bytes 262176 | tf_op jit(solution)/shard_map/all_to_all | solution.py:34
  (91 shorter events, 24.8 us)
Async XLA Ops:
  0.6 30.8 %copy-start = (bf16[1,2048,64]{1,2,0:T(8,128)(2,1)S(1)}, bf16[1,2048,64]{1,2,0:T(8,128)(2,1)}, u32[]{:S(2)}) copy-start(bf16[1,2048,64]{1,2,0:T(8,128)(2,1)} %param.12) | copy-start | bytes 786436
  0.6 9.3 %copy-start.18 = (bf16[64,512]{1,0:T(8,128)(2,1)S(1)}, bf16[64,512]{1,0:T(8,128)(2,1)}, u32[]{:S(2)}) copy-start(bf16[64,512]{1,0:T(8,128)(2,1)} %param.7) | copy-start | bytes 196612
  0.7 7.3 %copy-start.2 = (bf16[1,5,64,512]{3,2,1,0:T(8,128)(2,1)S(1)}, bf16[1,5,64,512]{3,2,1,0:T(8,128)(2,1)}, u32[]{:S(2)}) copy-start(bf16[1,5,64,512]{3,2,1,0:T(8,128)(2,1)} %param.8) | copy-start | bytes 983044
  0.7 9.2 %copy-start.16 = (bf16[512,256]{1,0:T(8,128)(2,1)S(1)}, bf16[512,256]{1,0:T(8,128)(2,1)}, u32[]{:S(2)}) copy-start(bf16[512,256]{1,0:T(8,128)(2,1)} %param.10) | copy-start | bytes 786436
  2.3 13.8 %all-to-all-start = ((bf16[4,64,512]{2,1,0:T(8,128)(2,1)}), bf16[4,64,512]{2,1,0:T(8,128)(2,1)S(1)}, u32[]{:S(2)}, u32[]{:S(2)}) async-start(bf16[4,64,512]{2,1,0:T(8,128)(2,1)} %broadcast_in_dim.28), calls=%async_computation | async-start | bytes 524288 | tf_op jit(solution)/shard_map/all_to_all | solution.py:34
  8.0 3.6 %collective-permute-start = (bf16[352,512]{1,0:T(8,128)(2,1)S(1)}, bf16[352,512]{1,0:T(8,128)(2,1)S(1)}, u32[]{:S(2)}, u32[]{:S(2)}) collective-permute-start(bf16[352,512]{1,0:T(8,128)(2,1)S(1)} %maximum_maximum_fusion), channel_id=1, source_target_pairs={{0,16},{16,0},{1,17},{17,1},{2,18},{18,2},{3,19},{19,3},{4,20},{20... | collective-permute-start | bytes 1081352 | tf_op jit(solution)/shard_map/ppermute | solution.py:42
  16.1 24.1 %copy-start.22 = (s32[5]{0:T(128)S(1)}, s32[5]{0:T(128)}, u32[]{:S(2)}) copy-start(s32[5]{0:T(128)} %constant.39.clone) | copy-start | bytes 64
  16.1 24.1 %copy-start.21 = (s32[1,5]{1,0:T(1,128)S(1)}, s32[1,5]{1,0:T(1,128)}, u32[]{:S(2)}) copy-start(s32[1,5]{1,0:T(1,128)} %param.9) | copy-start | bytes 64
  17.0 30.9 %all-to-all-start.1 = ((bf16[16,64,256]{2,1,0:T(8,128)(2,1)}), bf16[16,64,256]{2,1,0:T(8,128)(2,1)S(1)}, u32[]{:S(2)}, u32[]{:S(2)}) async-start(bf16[16,64,256]{2,1,0:T(8,128)(2,1)} %broadcast_in_dim.29), calls=%async_computation.1 | async-start | bytes 1048576 | tf_op jit(solution)/shard_map/all_to_all | solution.py:34
  31.5 17.5 %collective-permute-start.1 = (bf16[256,512]{1,0:T(8,128)(2,1)S(1)}, bf16[256,512]{1,0:T(8,128)(2,1)S(1)}, u32[]{:S(2)}, u32[]{:S(2)}) collective-permute-start(bf16[256,512]{1,0:T(8,128)(2,1)S(1)} %bitcast.38), channel_id=1, source_target_pairs={{0,128},{128,256},{256,384},{384,0},{1,129},{129,257},{257,385},{3... | collective-permute-start | bytes 786440 | tf_op jit(solution)/shard_map/ppermute | solution.py:52
  33.9 15.1 %collective-permute-start.2 = (bf16[256,512]{1,0:T(8,128)(2,1)S(1)}, bf16[256,512]{1,0:T(8,128)(2,1)S(1)}, u32[]{:S(2)}, u32[]{:S(2)}) collective-permute-start(bf16[256,512]{1,0:T(8,128)(2,1)S(1)} %bitcast.39), channel_id=1, source_target_pairs={{0,256},{128,384},{256,0},{384,128},{1,257},{129,385},{257,1},{385... | collective-permute-start | bytes 786440 | tf_op jit(solution)/shard_map/ppermute | solution.py:52
  38.3 11.1 %collective-permute-start.3 = (bf16[256,512]{1,0:T(8,128)(2,1)S(1)}, bf16[256,512]{1,0:T(8,128)(2,1)S(1)}, u32[]{:S(2)}, u32[]{:S(2)}) collective-permute-start(bf16[256,512]{1,0:T(8,128)(2,1)S(1)} %bitcast.40), channel_id=1, source_target_pairs={{0,384},{128,0},{256,128},{384,256},{1,385},{129,1},{257,129},{385... | collective-permute-start | bytes 786440 | tf_op jit(solution)/shard_map/ppermute | solution.py:52
  52.3 26.7 %copy-start.3 = (bf16[256,1,64]{0,2,1:T(8,128)(2,1)S(1)}, bf16[256,1,64]{0,2,1:T(8,128)(2,1)}, u32[]{:S(2)}) copy-start(bf16[256,1,64]{0,2,1:T(8,128)(2,1)} %param.11) | copy-start | bytes 98308
  53.1 25.8 %all-to-all-start.2 = ((bf16[16,64,384]{2,1,0:T(8,128)(2,1)}), bf16[16,64,384]{2,1,0:T(8,128)(2,1)S(1)}, u32[]{:S(2)}, u32[]{:S(2)}) async-start(bf16[16,64,384]{2,1,0:T(8,128)(2,1)} %pad_maximum_fusion), calls=%async_computation.2 | async-start | bytes 1572864 | tf_op jit(solution)/shard_map/all_to_all | solution.py:34
  60.5 18.8 %collective-permute-start.4 = (bf16[1024,128]{1,0:T(8,128)(2,1)}, bf16[1024,128]{1,0:T(8,128)(2,1)S(1)}, u32[]{:S(2)}, u32[]{:S(2)}) collective-permute-start(bf16[1024,128]{1,0:T(8,128)(2,1)} %copy-done.15), channel_id=1, source_target_pairs={{0,1},{1,0},{2,3},{3,2},{4,5},{5,4},{6,7},{7,6},{8,9},{9,8},{10,11... | collective-permute-start | bytes 786440 | tf_op jit(solution)/shard_map/ppermute | solution.py:48
  63.5 25.3 %collective-permute-start.5 = (bf16[1024,128]{1,0:T(8,128)(2,1)}, bf16[1024,128]{1,0:T(8,128)(2,1)}, u32[]{:S(2)}, u32[]{:S(2)}) collective-permute-start(bf16[1024,128]{1,0:T(8,128)(2,1)} %copy-done.14), channel_id=1, source_target_pairs={{0,2},{1,3},{2,0},{3,1},{4,6},{5,7},{6,4},{7,5},{8,10},{9,11},{10,... | collective-permute-start | bytes 786440 | tf_op jit(solution)/shard_map/ppermute | solution.py:48
  67.1 21.8 %collective-permute-start.6 = (bf16[1024,128]{1,0:T(8,128)(2,1)}, bf16[1024,128]{1,0:T(8,128)(2,1)}, u32[]{:S(2)}, u32[]{:S(2)}) collective-permute-start(bf16[1024,128]{1,0:T(8,128)(2,1)} %copy-done.13), channel_id=1, source_target_pairs={{0,4},{1,5},{2,6},{3,7},{4,0},{5,1},{6,2},{7,3},{8,12},{9,13},{10,... | collective-permute-start | bytes 786440 | tf_op jit(solution)/shard_map/ppermute | solution.py:48
  72.3 16.5 %collective-permute-start.7 = (bf16[1024,128]{1,0:T(8,128)(2,1)}, bf16[1024,128]{1,0:T(8,128)(2,1)}, u32[]{:S(2)}, u32[]{:S(2)}) collective-permute-start(bf16[1024,128]{1,0:T(8,128)(2,1)} %copy-done.12), channel_id=1, source_target_pairs={{0,8},{8,0},{1,9},{9,1},{2,10},{10,2},{3,11},{11,3},{4,12},{12,4},... | collective-permute-start | bytes 786440 | tf_op jit(solution)/shard_map/ppermute | solution.py:47
  91.3 44.5 %copy-start.6 = (bf16[1024,128]{1,0:T(8,128)(2,1)}, bf16[1024,128]{1,0:T(8,128)(2,1)S(1)}, u32[]{:S(2)}) copy-start(bf16[1024,128]{1,0:T(8,128)(2,1)S(1)} %get-tuple-element.76.a) | copy-start | bytes 786436
  91.3 30.0 %all-to-all-start.3 = ((bf16[32,32,256]{2,1,0:T(8,128)(2,1)}), bf16[32,32,256]{2,1,0:T(8,128)(2,1)}, u32[]{:S(2)}, u32[]{:S(2)}) async-start(bf16[32,32,256]{2,1,0:T(8,128)(2,1)} %bitcast.13), calls=%async_computation.3 | async-start | bytes 1048576 | tf_op jit(solution)/shard_map/all_to_all | solution.py:34
  101.3 34.5 %collective-permute-start.8 = (bf16[1024,128]{1,0:T(8,128)(2,1)S(1)}, bf16[1024,128]{1,0:T(8,128)(2,1)S(1)}, u32[]{:S(2)}, u32[]{:S(2)}) collective-permute-start(bf16[1024,128]{1,0:T(8,128)(2,1)S(1)} %get-tuple-element.76.a), channel_id=1, source_target_pairs={{0,1},{1,0},{2,3},{3,2},{4,5},{5,4},{6,7},{7,6},{8,9},{9,8},{10,11... | collective-permute-start | bytes 786440 | tf_op jit(solution)/shard_map/ppermute | solution.py:48
  104.6 31.1 %collective-permute-start.9 = (bf16[1024,128]{1,0:T(8,128)(2,1)S(1)}, bf16[1024,128]{1,0:T(8,128)(2,1)S(1)}, u32[]{:S(2)}, u32[]{:S(2)}) collective-permute-start(bf16[1024,128]{1,0:T(8,128)(2,1)S(1)} %get-tuple-element.76.a), channel_id=1, source_target_pairs={{0,2},{1,3},{2,0},{3,1},{4,6},{5,7},{6,4},{7,5},{8,10},{9,11},{10,... | collective-permute-start | bytes 786440 | tf_op jit(solution)/shard_map/ppermute | solution.py:48
  108.9 26.9 %collective-permute-start.10 = (bf16[1024,128]{1,0:T(8,128)(2,1)S(1)}, bf16[1024,128]{1,0:T(8,128)(2,1)}, u32[]{:S(2)}, u32[]{:S(2)}) collective-permute-start(bf16[1024,128]{1,0:T(8,128)(2,1)S(1)} %get-tuple-element.76.a), channel_id=1, source_target_pairs={{0,4},{1,5},{2,6},{3,7},{4,0},{5,1},{6,2},{7,3},{8,12},{9,13},{10,... | collective-permute-start | bytes 786440 | tf_op jit(solution)/shard_map/ppermute | solution.py:48
  114.0 21.8 %collective-permute-start.11 = (bf16[1024,128]{1,0:T(8,128)(2,1)S(1)}, bf16[1024,128]{1,0:T(8,128)(2,1)}, u32[]{:S(2)}, u32[]{:S(2)}) collective-permute-start(bf16[1024,128]{1,0:T(8,128)(2,1)S(1)} %get-tuple-element.76.a), channel_id=1, source_target_pairs={{0,8},{8,0},{1,9},{9,1},{2,10},{10,2},{3,11},{11,3},{4,12},{12,4},... | collective-permute-start | bytes 786440 | tf_op jit(solution)/shard_map/ppermute | solution.py:47
  139.3 19.9 %collective-permute-start.14 = (bf16[256,512]{1,0:T(8,128)(2,1)}, bf16[256,512]{1,0:T(8,128)(2,1)S(1)}, u32[]{:S(2)}, u32[]{:S(2)}) collective-permute-start(bf16[256,512]{1,0:T(8,128)(2,1)} %get-tuple-element.73), channel_id=1, source_target_pairs={{0,384},{128,0},{256,128},{384,256},{1,385},{129,1},{257,129},{385... | collective-permute-start | bytes 786440 | tf_op jit(solution)/shard_map/ppermute | solution.py:52
  142.1 17.3 %collective-permute-start.13 = (bf16[256,512]{1,0:T(8,128)(2,1)}, bf16[256,512]{1,0:T(8,128)(2,1)S(1)}, u32[]{:S(2)}, u32[]{:S(2)}) collective-permute-start(bf16[256,512]{1,0:T(8,128)(2,1)} %get-tuple-element.72), channel_id=1, source_target_pairs={{0,256},{128,384},{256,0},{384,128},{1,257},{129,385},{257,1},{385... | collective-permute-start | bytes 786440 | tf_op jit(solution)/shard_map/ppermute | solution.py:52
  145.1 15.5 %collective-permute-start.12 = (bf16[256,512]{1,0:T(8,128)(2,1)}, bf16[256,512]{1,0:T(8,128)(2,1)}, u32[]{:S(2)}, u32[]{:S(2)}) collective-permute-start(bf16[256,512]{1,0:T(8,128)(2,1)} %get-tuple-element.71), channel_id=1, source_target_pairs={{0,128},{128,256},{256,384},{384,0},{1,129},{129,257},{257,385},{3... | collective-permute-start | bytes 786440 | tf_op jit(solution)/shard_map/ppermute | solution.py:52
  150.0 24.0 %all-to-all-start.5 = ((bf16[32,32,256]{2,1,0:T(8,128)(2,1)}), bf16[32,32,256]{2,1,0:T(8,128)(2,1)S(1)}, u32[]{:S(2)}, u32[]{:S(2)}) async-start(bf16[32,32,256]{2,1,0:T(8,128)(2,1)} %broadcast_in_dim.56), calls=%async_computation.5 | async-start | bytes 1048576 | tf_op jit(solution)/shard_map/all_to_all | solution.py:34
  167.5 4.4 %collective-permute-start.15 = (f32[352,512]{1,0:T(8,128)}, f32[352,512]{1,0:T(8,128)}, u32[]{:S(2)}, u32[]{:S(2)}) collective-permute-start(f32[352,512]{1,0:T(8,128)} %get-tuple-element.86), channel_id=1, source_target_pairs={{0,16},{16,0},{1,17},{17,1},{2,18},{18,2},{3,19},{19,3},{4,20},{20... | collective-permute-start | bytes 2162696 | tf_op jit(solution)/shard_map/ppermute | solution.py:42
  174.0 13.8 %all-to-all-start.6 = ((bf16[4,64,512]{2,1,0:T(8,128)(2,1)}), bf16[4,64,512]{2,1,0:T(8,128)(2,1)S(1)}, u32[]{:S(2)}, u32[]{:S(2)}) async-start(bf16[4,64,512]{2,1,0:T(8,128)(2,1)} %bitcast.50), calls=%async_computation.6 | async-start | bytes 524288 | tf_op jit(solution)/shard_map/all_to_all | solution.py:34
  179.3 8.5 %copy-start.17 = (bf16[512,256]{1,0:T(8,128)(2,1)S(1)}, bf16[512,256]{1,0:T(8,128)(2,1)}, u32[]{:S(2)}) copy-start(bf16[512,256]{1,0:T(8,128)(2,1)} %param.10) | copy-start | bytes 786436
  179.8 8.8 %collective-permute-start.16 = (f32[512,256]{1,0:T(8,128)S(1)}, f32[512,256]{1,0:T(8,128)S(1)}, u32[]{:S(2)}, u32[]{:S(2)}) collective-permute-start(f32[512,256]{1,0:T(8,128)S(1)} %shard_map.108), channel_id=1, source_target_pairs={{0,16},{16,0},{1,17},{17,1},{2,18},{18,2},{3,19},{19,3},{4,20},{20... | collective-permute-start | bytes 1572872 | tf_op jit(solution)/shard_map/ppermute | solution.py:42
  (14 other events, 15.3 us)
